TPU v7x, 512 devices: a whole 4x8x8 slice. The times are simulated.
512 devices in a mesh: slab: 32 (over y_lo, x, core), filt: 16 (over y_hi, z).
Axes of the slice: x: 4, y: 8 (y_hi: 2, y_lo: 4; y = y_hi * 4 + y_lo), z: 8, core: 2. Of those that a mesh axis runs over, the one named last changes fastest.
Arguments:
- volume: bfloat16 [512, 32, 1024], P('filt', 'slab'), may hold values from -6 to 6
- kernel: bfloat16 [27, 512, 512], P(None, 'filt'), may hold values from -0.0546875 to 0.0546875
- channel_bias: float32 [512], P('filt'), may hold values from -3 to 3
Outputs:
- feature_out: bfloat16 [512, 32, 1024], P('filt', 'slab')
All inputs are finite; a program needn't handle non-finite values.
Results may differ from a plain program's by a relative error of at most 0.001.
Values may be sent and summed in bfloat16 or wider, within the bound.
No kernel may reach another device: no remote copies, remote signals or barrier semaphores. Data moves between devices by JAX's collectives and lax.ppermute only.
A program may use at most 128 MiB of HBM per device.

v0:
```python
import jax
import jax.numpy as jnp
from jax import lax
from jax.sharding import PartitionSpec as P

PLANES = 1
SIDE = 32


def with_halo(block, sides, width):
    for axis, dim in sides:
        count = lax.axis_size(axis)
        forward = [(i, i + 1) for i in range(count - 1)]
        backward = [(target, source) for source, target in forward]
        low = lax.ppermute(
            lax.slice_in_dim(block, block.shape[dim] - width, None, axis=dim), axis, forward
        )
        high = lax.ppermute(lax.slice_in_dim(block, 0, width, axis=dim), axis, backward)
        block = jnp.concatenate([low, block, high], axis=dim)
    return block


def add_taps(running, bordered, weight_cols):
    channels = bordered.shape[0]
    planes_here = bordered.shape[1] - 2
    cells = bordered.shape[2]
    out_rows = weight_cols.shape[1]
    column = lax.broadcasted_iota(jnp.int32, (1, 1, 1, cells), 3) % SIDE
    for plane_off in range(3):
        weight_group = weight_cols[9 * plane_off : 9 * plane_off + 9].reshape(
            9 * out_rows, channels
        )
        block = bordered[:, plane_off : plane_off + planes_here, :].reshape(
            channels, planes_here * cells
        )
        product = jnp.dot(weight_group, block, preferred_element_type=jnp.float32)
        product = product.reshape(9, out_rows, planes_here, cells)
        padded = jnp.pad(product, ((0, 0), (0, 0), (0, 0), (SIDE + 1, SIDE + 1)))
        for row_off in range(3):
            for col_off in range(3):
                start = row_off * SIDE + col_off
                moved = padded[
                    3 * row_off + col_off : 3 * row_off + col_off + 1, :, :, start : start + cells
                ]
                if col_off == 0:
                    moved = jnp.where(column >= 1, moved, jnp.zeros_like(moved))
                elif col_off == 2:
                    moved = jnp.where(column <= SIDE - 2, moved, jnp.zeros_like(moved))
                running = running + moved.reshape(out_rows, planes_here * cells)
    return running


def on_device(volume, kernel, channel_bias):
    own_out = kernel.shape[1]
    plane_cells = volume.shape[2]
    initial = jnp.zeros((own_out, PLANES * plane_cells), jnp.float32)
    gathered = lax.all_gather(volume, "filt", axis=0, tiled=True)
    bordered = with_halo(gathered, (("slab", 1),), 1)
    summed = add_taps(initial, bordered, kernel)
    summed = summed + channel_bias[:, None]
    return summed.reshape(own_out, PLANES, plane_cells).astype(jnp.bfloat16)


def solution(mesh):
    return jax.shard_map(
        on_device,
        mesh=mesh,
        in_specs=(P("filt", "slab", None), P(None, "filt", None), P("filt")),
        out_specs=P("filt", "slab", None),
        check_vma=False,
    )
```

profile of v0, /device:TPU:7, one launch (start us, length us, event | category | flops | bytes accessed | tf_op | source)
XLA Modules:
  0.0 137.9 jit_solution(4008405847262415667)
XLA Ops:
  6.5 0.0 copy-start
  6.5 0.0 all-gather.2.cloned.1.call-start
  6.5 0.7 all-gather.2.cloned.1.call-update
  7.3 93.2 %all-gather.2.cloned.1.call-done = bf16[512,1,1024]{2,0,1:T(8,128)(2,1)} async-done(((bf16[32,1,1024]{2,0,1:T(8,128)(2,1)}), bf16[512,1,1024]{2,0,1:T(8,128)(2,1)}) %all-gather.2.cloned.1.call-update) | async-done | bytes 1048592 | tf_op jit(solution)/shard_map/all_gather | solution.py:57
  100.4 10.2 %collective-permute-start = (bf16[512,1,1024]{2,0,1:T(8,128)(2,1)}, bf16[512,1,1024]{2,0,1:T(8,128)(2,1)S(1)}, u32[]{:S(2)}, u32[]{:S(2)}) collective-permute-start(bf16[512,1,1024]{2,0,1:T(8,128)(2,1)} %all-gather.2.cloned.1.call-done), channel_id=1, source_target_pairs={{0,16},{16,32},{32,48},{48,64},{64,80},{80,96},{96,112},{112,128},... | collective-permute-start | bytes 3145736 | tf_op jit(solution)/shard_map/ppermute | solution.py:15
  110.6 1.9 %collective-permute-start.1 = (bf16[512,1,1024]{2,0,1:T(8,128)(2,1)}, bf16[512,1,1024]{2,0,1:T(8,128)(2,1)S(1)}, u32[]{:S(2)}, u32[]{:S(2)}) collective-permute-start(bf16[512,1,1024]{2,0,1:T(8,128)(2,1)} %all-gather.2.cloned.1.call-done), channel_id=1, source_target_pairs={{16,0},{32,16},{48,32},{64,48},{80,64},{96,80},{112,96},{128,112},... | collective-permute-start | bytes 3145736 | tf_op jit(solution)/shard_map/ppermute | solution.py:18
  112.5 0.0 copy-done
  112.5 1.7 %fusion.2 = f32[9,32,1024]{2,1,0:T(8,128)S(1)} fusion(bf16[27,32,512]{2,1,0:T(8,128)(2,1)S(1)} %copy-done, bf16[512,1,1024]{2,0,1:T(8,128)(2,1)} %all-gather.2.cloned.1.call-done), kind=kOutput, calls=%fused_computation.26 | convolution fusion | flops 301989888 | bytes 3112960 | tf_op jit(solution)/shard_map/dot_general | solution.py:36
  114.2 8.4 %collective-permute-done = bf16[512,1,1024]{2,0,1:T(8,128)(2,1)S(1)} collective-permute-done((bf16[512,1,1024]{2,0,1:T(8,128)(2,1)}, bf16[512,1,1024]{2,0,1:T(8,128)(2,1)S(1)}, u32[]{:S(2)}, u32[]{:S(2)}) %collective-permute-start) | collective-permute-done | bytes 1048608 | tf_op jit(solution)/shard_map/ppermute | solution.py:15
  122.6 0.5 fusion.4
  123.1 0.0 copy-start.1
  123.1 5.9 %collective-permute-done.1 = bf16[512,1,1024]{2,0,1:T(8,128)(2,1)S(1)} collective-permute-done((bf16[512,1,1024]{2,0,1:T(8,128)(2,1)}, bf16[512,1,1024]{2,0,1:T(8,128)(2,1)S(1)}, u32[]{:S(2)}, u32[]{:S(2)}) %collective-permute-start.1) | collective-permute-done | bytes 1048608 | tf_op jit(solution)/shard_map/ppermute | solution.py:18
  129.0 0.5 fusion
  129.5 0.0 copy-done.1
  129.5 1.5 %add_convert_fusion = bf16[32,1,1024]{2,0,1:T(8,128)(2,1)} fusion(f32[9,32,1,1024]{3,1,2,0:T(8,128)S(1)} %bitcast.230, f32[9,32,1024]{2,1,0:T(8,128)S(1)} %fusion, f32[9,32,1,1024]{3,1,2,0:T(8,128)S(1)} %bitcast.228, f32[9,32,1024]{2,1,0:T(8,128)S(1)} %fusion.2, f32[9,32,1,1024]{3,1,2,0:T(8,128)S(1)} %bitcast.229, f32[9,32,1024]{2,1,0:T(8,128)S(1)} %fusion.4, ...), kind=kLoop, calls=%fused_computation.98 | loop fusion | flops 1507328 | bytes 3999872 | tf_op jit(solution)/shard_map/convert_element_type | solution.py:61
  (1 shorter events, 0.0 us)
Async XLA Ops:
  6.5 106.0 %copy-start = (bf16[27,32,512]{2,1,0:T(8,128)(2,1)S(1)}, bf16[27,32,512]{2,1,0:T(8,128)(2,1)}, u32[]{:S(2)}) copy-start(bf16[27,32,512]{2,1,0:T(8,128)(2,1)} %param.4) | copy-start | bytes 2654212
  6.5 93.9 %all-gather.2.cloned.1.call-start = ((), (), s32[]{:S(2)}) async-start(), calls=%async_computation | async-start | bytes 1114112 | tf_op jit(solution)/shard_map/all_gather | solution.py:57
  100.4 22.2 %collective-permute-start = (bf16[512,1,1024]{2,0,1:T(8,128)(2,1)}, bf16[512,1,1024]{2,0,1:T(8,128)(2,1)S(1)}, u32[]{:S(2)}, u32[]{:S(2)}) collective-permute-start(bf16[512,1,1024]{2,0,1:T(8,128)(2,1)} %all-gather.2.cloned.1.call-done), channel_id=1, source_target_pairs={{0,16},{16,32},{32,48},{48,64},{64,80},{80,96},{96,112},{112,128},... | collective-permute-start | bytes 3145736 | tf_op jit(solution)/shard_map/ppermute | solution.py:15
  110.6 18.4 %collective-permute-start.1 = (bf16[512,1,1024]{2,0,1:T(8,128)(2,1)}, bf16[512,1,1024]{2,0,1:T(8,128)(2,1)S(1)}, u32[]{:S(2)}, u32[]{:S(2)}) collective-permute-start(bf16[512,1,1024]{2,0,1:T(8,128)(2,1)} %all-gather.2.cloned.1.call-done), channel_id=1, source_target_pairs={{16,0},{32,16},{48,32},{64,48},{80,64},{96,80},{112,96},{128,112},... | collective-permute-start | bytes 3145736 | tf_op jit(solution)/shard_map/ppermute | solution.py:18
  123.1 6.4 %copy-start.1 = (f32[32]{0:T(128)S(1)}, f32[32]{0:T(128)}, u32[]{:S(2)}) copy-start(f32[32]{0:T(128)} %param.5) | copy-start | bytes 388
Sparse Core Ops, SparseCore 0:
  10.5 89.8 all-gather.1
where the time goes:
time: 138 us
  waiting for transfers between devices  108 us (78%)
  between operations  13.5 us (10%)
  starting transfers between devices  12.1 us (9%)
  matrix products  2.65 us (2%)
  other arithmetic  1.52 us (1%)
    all_gather x1, waiting for transfers between devices, on_device(): gathered = lax.all_gather(volume, 'filt', axis=0, tiled=True)  93.2 us
    ppermute x1, starting transfers between devices, with_halo(): lax.ppermute(lax.slice_in_dim(block, block.shape[dim] - width, None, axis...  10.2 us
    ppermute x1, waiting for transfers between devices, with_halo(): lax.ppermute(lax.slice_in_dim(block, block.shape[dim] - width, None, axis...  8.39 us
    ppermute x1, waiting for transfers between devices, with_halo(): lax.ppermute(lax.slice_in_dim(block, 0, width, axis=dim), axis, backward)  5.9 us
  transfers between devices with their start and end apart: 3, of which 3 were waited for; matrix products, arithmetic and copies ran while one was open for 2% of the time, Pallas kernels for 0%

commit v1 on v0

v1 whole, which is shorter than its diff:
```python
import jax
import jax.numpy as jnp
from jax import lax
from jax.experimental import pallas as pl
from jax.experimental.pallas import tpu as pltpu
from jax.sharding import PartitionSpec as P

SIDE = 32


def shifted_rows(value, rows):
    cells = value.shape[1]
    place = lax.broadcasted_iota(jnp.int32, value.shape, 1)
    moved = pltpu.roll(value, (rows * SIDE) % cells, 1)
    inside = place >= rows * SIDE if rows > 0 else place < cells + rows * SIDE
    return jnp.where(inside, moved, 0.0)


def shifted_cols(value, cols):
    cells = value.shape[1]
    column = lax.broadcasted_iota(jnp.int32, value.shape, 1) % SIDE
    moved = pltpu.roll(value, cols % cells, 1)
    inside = column >= 1 if cols > 0 else column <= SIDE - 2
    return jnp.where(inside, moved, 0.0)


def taps_kernel(parity_ref, plane_ref, weight_ref, bias_ref, centre_ref, pair_ref, next_ref):
    out_rows = weight_ref.shape[1]
    plane = plane_ref[...]
    sums = []
    for plane_off in range(3):
        group = weight_ref[9 * plane_off : 9 * plane_off + 9].reshape(
            9 * out_rows, weight_ref.shape[2]
        )
        product = jnp.dot(group, plane, preferred_element_type=jnp.float32)
        taps = [
            product[tap * out_rows : (tap + 1) * out_rows] for tap in range(9)
        ]
        by_col = [
            taps[3 + col] + shifted_rows(taps[col], 1) + shifted_rows(taps[6 + col], -1)
            for col in range(3)
        ]
        sums.append(
            by_col[1] + shifted_cols(by_col[0], 1) + shifted_cols(by_col[2], -1)
        )
    above, own, below = sums
    even = parity_ref[0] == 0
    centre_ref[...] = own + bias_ref[...]
    pair_ref[...] = jnp.where(even, above, below)
    next_ref[...] = jnp.where(even, below, above)


def taps(parity, plane, weights, bias):
    out_rows = weights.shape[1]
    cells = plane.shape[1]
    out = jax.ShapeDtypeStruct((out_rows, cells), jnp.float32)
    vmem = pl.BlockSpec(memory_space=pltpu.VMEM)
    return pl.pallas_call(
        taps_kernel,
        out_shape=(out, out, out),
        in_specs=[pl.BlockSpec(memory_space=pltpu.SMEM), vmem, vmem, vmem],
        out_specs=(vmem, vmem, vmem),
        compiler_params=pltpu.CompilerParams(vmem_limit_bytes=40 * 1024 * 1024),
    )(parity, plane, weights, bias)


def on_device(volume, kernel, channel_bias):
    own_in, planes, cells = volume.shape
    own_out = kernel.shape[1]
    filt = lax.axis_size("filt")
    slabs = lax.axis_size("slab")
    copies = jnp.broadcast_to(volume.reshape(1, own_in, cells), (filt, own_in, cells))
    gathered = lax.all_to_all(copies, "filt", 0, 0)
    plane = gathered.reshape(filt * own_in, cells)
    parity = (lax.axis_index("slab") % 2).reshape(1)
    centre, to_pair, to_next = taps(parity, plane, kernel, channel_bias[:, None])
    pairs = [(i, i ^ 1) for i in range(slabs)]
    nexts = [(i, i + 1) for i in range(1, slabs - 1, 2)]
    nexts += [(target, source) for source, target in nexts]
    from_next = lax.ppermute(to_next, "slab", nexts)
    from_pair = lax.ppermute(to_pair, "slab", pairs)
    summed = centre + from_pair + from_next
    return summed.reshape(own_out, planes, cells).astype(jnp.bfloat16)


def solution(mesh):
    return jax.shard_map(
        on_device,
        mesh=mesh,
        in_specs=(P("filt", "slab", None), P(None, "filt", None), P("filt")),
        out_specs=P("filt", "slab", None),
        check_vma=False,
    )
```

time: 138 us -> 63.5 us (0.46)
  the two profiles are of different devices: /device:TPU:7 before, /device:TPU:15 now
where the time goes in v1:
time: 63.5 us; the launch traced here: 63.3 us
  waiting for transfers between devices  39 us (61%)
  starting transfers between devices  19.5 us (31%)
  local copies, waits for them, and re-layouts  2.68 us (4%)
  Pallas kernels  1.38 us (2%)
  other arithmetic  0.65 us (1%)
    all_to_all x1, waiting for transfers between devices, on_device(): gathered = lax.all_to_all(copies, 'filt', 0, 0)  32.5 us
    all_to_all x1, starting transfers between devices, on_device(): gathered = lax.all_to_all(copies, 'filt', 0, 0)  14.6 us
    ppermute x1, waiting for transfers between devices, on_device(): from_next = lax.ppermute(to_next, 'slab', nexts)  6.46 us
    ppermute x1, starting transfers between devices, on_device(): from_pair = lax.ppermute(to_pair, 'slab', pairs)  2.93 us
    broadcast_in_dim x1, local copies, waits for them, and re-layouts, on_device(): jnp.broadcast_to(volume.reshape(1, own_in, cells), (filt, own_in, cells))  1.94 us
    ppermute x1, starting transfers between devices, on_device(): from_next = lax.ppermute(to_next, 'slab', nexts)  1.92 us
    pallas_call x1, Pallas kernels, taps(): pl.pallas_call(taps_kernel, out_shape=(out, out, out), in_specs=[pl.Block...  1.38 us
  transfers between devices with their start and end apart: 3, of which 2 were waited for; matrix products, arithmetic and copies ran while one was open for 0% of the time, Pallas kernels for 0%

profile of v1, /device:TPU:15, one launch (start us, length us, event | category | flops | bytes accessed | tf_op | source)
XLA Modules:
  0.0 63.3 jit_solution(3309824387307697489)
XLA Ops:
  0.0 1.9 %broadcast_in_dim.11 = bf16[16,32,1024]{2,1,0:T(8,128)(2,1)} broadcast(bf16[32,1024]{1,0:T(8,128)(2,1)} %bitcast.7), dimensions={1,2} | broadcast | bytes 1114112 | tf_op jit(solution)/shard_map/broadcast_in_dim | solution.py:72
  1.9 0.0 copy-start
  1.9 14.6 %all-to-all-start = ((bf16[16,32,1024]{2,1,0:T(8,128)(2,1)}), bf16[16,32,1024]{2,1,0:T(8,128)(2,1)S(1)}, u32[]{:S(2)}, u32[]{:S(2)}) async-start(bf16[16,32,1024]{2,1,0:T(8,128)(2,1)} %broadcast_in_dim.11), calls=%async_computation | async-start | bytes 2097152 | tf_op jit(solution)/shard_map/all_to_all | solution.py:73
  16.6 0.0 copy-start.1
  16.6 0.6 %copy-done.1 = f32[32]{0:T(128)S(1)} copy-done((f32[32]{0:T(128)S(1)}, f32[32]{0:T(128)}, u32[]{:S(2)}) %copy-start.1) | copy-done | bytes 152
  17.2 0.1 copy.4.bias_ref
  17.3 32.5 %all-to-all-done = bf16[16,32,1024]{2,1,0:T(8,128)(2,1)S(1)} async-done(((bf16[16,32,1024]{2,1,0:T(8,128)(2,1)}), bf16[16,32,1024]{2,1,0:T(8,128)(2,1)S(1)}, u32[]{:S(2)}, u32[]{:S(2)}) %all-to-all-start) | async-done | bytes 1048608 | tf_op jit(solution)/shard_map/all_to_all | solution.py:73
  49.9 0.0 copy-done
  49.9 1.4 %shard_map.37 = (f32[32,1024]{1,0:T(8,128)S(1)}, f32[32,1024]{1,0:T(8,128)S(1)}, f32[32,1024]{1,0:T(8,128)S(1)}) custom-call(s32[1]{0:T(128)} %bitcast.parity_ref, bf16[512,1024]{1,0:T(8,128)(2,1)S(1)} %bitcast.6, bf16[27,32,512]{2,1,0:T(8,128)(2,1)S(1)} %copy-done, f32[32,1]{1,0:T(8,128)S(1)} %copy.4.bias_ref), custom_call_target="tpu_custom_call" | custom-call | tf_op jit(solution)/shard_map/pallas_call | solution.py:58
  51.3 2.9 %collective-permute-start = (f32[32,1024]{1,0:T(8,128)S(1)}, f32[32,1024]{1,0:T(8,128)S(1)}, u32[]{:S(2)}, u32[]{:S(2)}) collective-permute-start(f32[32,1024]{1,0:T(8,128)S(1)} %get-tuple-element.9), channel_id=1, source_target_pairs={{0,16},{16,0},{32,48},{48,32},{64,80},{80,64},{96,112},{112,96},{1... | collective-permute-start | bytes 393224 | tf_op jit(solution)/shard_map/ppermute | solution.py:81
  54.2 1.9 %collective-permute-start.1 = (f32[32,1024]{1,0:T(8,128)S(1)}, f32[32,1024]{1,0:T(8,128)S(1)}, u32[]{:S(2)}, u32[]{:S(2)}) collective-permute-start(f32[32,1024]{1,0:T(8,128)S(1)} %get-tuple-element.10), channel_id=1, source_target_pairs={{16,32},{48,64},{80,96},{112,128},{144,160},{176,192},{208,224},{2... | collective-permute-start | bytes 393224 | tf_op jit(solution)/shard_map/ppermute | solution.py:80
  56.1 0.0 collective-permute-done
  56.1 6.5 %collective-permute-done.1 = f32[32,1024]{1,0:T(8,128)S(1)} collective-permute-done((f32[32,1024]{1,0:T(8,128)S(1)}, f32[32,1024]{1,0:T(8,128)S(1)}, u32[]{:S(2)}, u32[]{:S(2)}) %collective-permute-start.1) | collective-permute-done | bytes 131104 | tf_op jit(solution)/shard_map/ppermute | solution.py:80
  62.6 0.7 %fusion = bf16[32,1,1024]{2,0,1:T(8,128)(2,1)} fusion(f32[32,1024]{1,0:T(8,128)S(1)} %collective-permute-done.1, f32[32,1024]{1,0:T(8,128)S(1)} %get-tuple-element.8, f32[32,1024]{1,0:T(8,128)S(1)} %collective-permute-done), kind=kLoop, calls=%fused_computation.1 | loop fusion | flops 98304 | bytes 458752 | tf_op jit(solution)/shard_map/convert_element_type | solution.py:83
Async XLA Ops:
  1.9 47.9 %copy-start = (bf16[27,32,512]{2,1,0:T(8,128)(2,1)S(1)}, bf16[27,32,512]{2,1,0:T(8,128)(2,1)}, u32[]{:S(2)}) copy-start(bf16[27,32,512]{2,1,0:T(8,128)(2,1)} %weight_ref.1) | copy-start | bytes 2654212
  1.9 47.9 %all-to-all-start = ((bf16[16,32,1024]{2,1,0:T(8,128)(2,1)}), bf16[16,32,1024]{2,1,0:T(8,128)(2,1)S(1)}, u32[]{:S(2)}, u32[]{:S(2)}) async-start(bf16[16,32,1024]{2,1,0:T(8,128)(2,1)} %broadcast_in_dim.11), calls=%async_computation | async-start | bytes 2097152 | tf_op jit(solution)/shard_map/all_to_all | solution.py:73
  16.6 0.7 %copy-start.1 = (f32[32]{0:T(128)S(1)}, f32[32]{0:T(128)}, u32[]{:S(2)}) copy-start(f32[32]{0:T(128)} %param.5) | copy-start | bytes 388
  51.3 4.9 %collective-permute-start = (f32[32,1024]{1,0:T(8,128)S(1)}, f32[32,1024]{1,0:T(8,128)S(1)}, u32[]{:S(2)}, u32[]{:S(2)}) collective-permute-start(f32[32,1024]{1,0:T(8,128)S(1)} %get-tuple-element.9), channel_id=1, source_target_pairs={{0,16},{16,0},{32,48},{48,32},{64,80},{80,64},{96,112},{112,96},{1... | collective-permute-start | bytes 393224 | tf_op jit(solution)/shard_map/ppermute | solution.py:81
  54.2 8.4 %collective-permute-start.1 = (f32[32,1024]{1,0:T(8,128)S(1)}, f32[32,1024]{1,0:T(8,128)S(1)}, u32[]{:S(2)}, u32[]{:S(2)}) collective-permute-start(f32[32,1024]{1,0:T(8,128)S(1)} %get-tuple-element.10), channel_id=1, source_target_pairs={{16,32},{48,64},{80,96},{112,128},{144,160},{176,192},{208,224},{2... | collective-permute-start | bytes 393224 | tf_op jit(solution)/shard_map/ppermute | solution.py:80

commit v2 on v1

v2 whole, which is shorter than its diff:
```python
import jax
import jax.numpy as jnp
from jax import lax
from jax.experimental import pallas as pl
from jax.experimental.pallas import tpu as pltpu
from jax.sharding import PartitionSpec as P

SIDE = 32


def shifted_rows(value, rows):
    cells = value.shape[1]
    place = lax.broadcasted_iota(jnp.int32, value.shape, 1)
    moved = pltpu.roll(value, (rows * SIDE) % cells, 1)
    inside = place >= rows * SIDE if rows > 0 else place < cells + rows * SIDE
    return jnp.where(inside, moved, 0.0)


def shifted_cols(value, cols):
    cells = value.shape[1]
    column = lax.broadcasted_iota(jnp.int32, value.shape, 1) % SIDE
    moved = pltpu.roll(value, cols % cells, 1)
    inside = column >= 1 if cols > 0 else column <= SIDE - 2
    return jnp.where(inside, moved, 0.0)


def plane_taps(plane, weight_ref, plane_off):
    out_rows, channels = weight_ref.shape[1:]
    group = weight_ref[pl.ds(9 * plane_off, 9)].reshape(9 * out_rows, channels)
    product = jnp.dot(group, plane, preferred_element_type=jnp.float32)
    taps = [product[tap * out_rows : (tap + 1) * out_rows] for tap in range(9)]
    by_col = [
        taps[3 + col] + shifted_rows(taps[col], 1) + shifted_rows(taps[6 + col], -1)
        for col in range(3)
    ]
    return by_col[1] + shifted_cols(by_col[0], 1) + shifted_cols(by_col[2], -1)


def next_kernel(odd_ref, plane_ref, weight_ref, next_ref):
    next_ref[...] = plane_taps(plane_ref[...], weight_ref, 2 - 2 * odd_ref[0])


def rest_kernel(odd_ref, plane_ref, weight_ref, pair_ref, centre_ref):
    plane = plane_ref[...]
    pair_ref[...] = plane_taps(plane, weight_ref, 2 * odd_ref[0])
    centre_ref[...] = plane_taps(plane, weight_ref, 1)


def copies_kernel(block_ref, copies_ref):
    block = block_ref[...]
    for i in range(copies_ref.shape[0]):
        copies_ref[i] = block


VMEM = pl.BlockSpec(memory_space=pltpu.VMEM)
SMEM = pl.BlockSpec(memory_space=pltpu.SMEM)
PARAMS = pltpu.CompilerParams(vmem_limit_bytes=40 * 1024 * 1024)


def add_kernel(first_ref, second_ref, out_ref):
    out_ref[...] = first_ref[...] + second_ref[...]


def added(first, second):
    return pl.pallas_call(
        add_kernel,
        out_shape=jax.ShapeDtypeStruct(first.shape, first.dtype),
        in_specs=[VMEM, VMEM],
        out_specs=VMEM,
        compiler_params=PARAMS,
        cost_estimate=pl.CostEstimate(flops=10**10, bytes_accessed=0, transcendentals=0),
    )(first, second)


def taps(body, outs, odd, plane, weights):
    out = jax.ShapeDtypeStruct((weights.shape[1], plane.shape[1]), jnp.float32)
    return pl.pallas_call(
        body,
        out_shape=(out,) * outs,
        in_specs=[SMEM, VMEM, VMEM],
        out_specs=(VMEM,) * outs,
        compiler_params=PARAMS,
    )(odd, plane, weights)


def copied(block, count):
    return pl.pallas_call(
        copies_kernel,
        out_shape=jax.ShapeDtypeStruct((count,) + block.shape, block.dtype),
        in_specs=[VMEM],
        out_specs=VMEM,
        compiler_params=PARAMS,
    )(block)


def on_device(volume, kernel, channel_bias):
    own_in, planes, cells = volume.shape
    own_out = kernel.shape[1]
    filt = lax.axis_size("filt")
    slabs = lax.axis_size("slab")
    copies = copied(volume.reshape(own_in, cells), filt)
    gathered = lax.all_to_all(copies, "filt", 0, 0)
    plane = gathered.reshape(filt * own_in, cells)
    odd = (lax.axis_index("slab") % 2).astype(jnp.int32).reshape(1)
    pairs = [(i, i ^ 1) for i in range(slabs)]
    nexts = [(i, i + 1) for i in range(1, slabs - 1, 2)]
    nexts += [(target, source) for source, target in nexts]
    (to_next,) = taps(next_kernel, 1, odd, plane, kernel)
    from_next = lax.ppermute(to_next, "slab", nexts)
    to_pair, centre = taps(rest_kernel, 2, odd, plane, kernel)
    from_pair = lax.ppermute(to_pair, "slab", pairs)
    summed = added(centre, from_next) + from_pair + channel_bias[:, None]
    return summed.reshape(own_out, planes, cells).astype(jnp.bfloat16)


def solution(mesh):
    return jax.shard_map(
        on_device,
        mesh=mesh,
        in_specs=(P("filt", "slab", None), P(None, "filt", None), P("filt")),
        out_specs=P("filt", "slab", None),
        check_vma=False,
    )
```

time: 63.5 us -> 60.9 us (0.959)
  the two profiles are of different devices: /device:TPU:15 before, /device:TPU:8 now
where the time goes in v2:
time: 60.9 us; the launch traced here: 60.6 us
  waiting for transfers between devices  35.3 us (58%)
  starting transfers between devices  20.3 us (33%)
  Pallas kernels  2.77 us (5%)
  local copies, waits for them, and re-layouts  1.47 us (2%)
  other arithmetic  0.7 us (1%)
    all_to_all x1, waiting for transfers between devices, on_device(): gathered = lax.all_to_all(copies, 'filt', 0, 0)  33.4 us
    all_to_all x1, starting transfers between devices, on_device(): gathered = lax.all_to_all(copies, 'filt', 0, 0)  14.9 us
    ppermute x1, starting transfers between devices, on_device(): from_pair = lax.ppermute(to_pair, 'slab', pairs)  3.5 us
    ppermute x1, waiting for transfers between devices, on_device(): from_next = lax.ppermute(to_next, 'slab', nexts)  1.93 us
    ppermute x1, starting transfers between devices, on_device(): from_next = lax.ppermute(to_next, 'slab', nexts)  1.92 us
    pallas_call x2, Pallas kernels, taps(): pl.pallas_call(body, out_shape=(out,) * outs, in_specs=[SMEM, VMEM, VMEM]...  1.68 us
    unnamed x6, local copies, waits for them, and re-layouts  1.47 us
  transfers between devices with their start and end apart: 3, of which 2 were waited for; matrix products, arithmetic and copies ran while one was open for 0% of the time, Pallas kernels for 2%

profile of v2, /device:TPU:8, one launch (start us, length us, event | category | flops | bytes accessed | tf_op | source)
XLA Modules:
  0.0 60.6 jit_solution(6778877646263186392)
XLA Ops:
  0.0 0.0 copy-start.1
  0.0 0.8 %copy-done.1 = bf16[32,1,1024]{2,0,1:T(8,128)(2,1)S(1)} copy-done((bf16[32,1,1024]{2,0,1:T(8,128)(2,1)S(1)}, bf16[32,1,1024]{2,0,1:T(8,128)(2,1)}, u32[]{:S(2)}) %copy-start.1) | copy-done | bytes 65560
  0.8 1.1 %shard_map.37 = bf16[16,32,1024]{2,1,0:T(8,128)(2,1)} custom-call(bf16[32,1024]{1,0:T(8,128)(2,1)S(1)} %bitcast.7), custom_call_target="tpu_custom_call" | custom-call | tf_op jit(solution)/shard_map/pallas_call | solution.py:87
  1.9 0.0 copy-start
  1.9 14.9 %all-to-all-start = ((bf16[16,32,1024]{2,1,0:T(8,128)(2,1)}), bf16[16,32,1024]{2,1,0:T(8,128)(2,1)S(1)}, u32[]{:S(2)}, u32[]{:S(2)}) async-start(bf16[16,32,1024]{2,1,0:T(8,128)(2,1)} %shard_map.37), calls=%async_computation | async-start | bytes 2097152 | tf_op jit(solution)/shard_map/all_to_all | solution.py:102
  16.8 33.4 %all-to-all-done = bf16[16,32,1024]{2,1,0:T(8,128)(2,1)S(1)} async-done(((bf16[16,32,1024]{2,1,0:T(8,128)(2,1)}), bf16[16,32,1024]{2,1,0:T(8,128)(2,1)S(1)}, u32[]{:S(2)}, u32[]{:S(2)}) %all-to-all-start) | async-done | bytes 1048608 | tf_op jit(solution)/shard_map/all_to_all | solution.py:102
  50.2 0.0 copy-done
  50.2 0.7 %shard_map.39 = f32[32,1024]{1,0:T(8,128)S(1)} custom-call(s32[1]{0:T(128)} %bitcast.odd_ref, bf16[512,1024]{1,0:T(8,128)(2,1)S(1)} %bitcast.5, bf16[27,32,512]{2,1,0:T(8,128)(2,1)S(1)} %copy-done), custom_call_target="tpu_custom_call" | custom-call | tf_op jit(solution)/shard_map/pallas_call | solution.py:77
  50.9 1.9 %collective-permute-start = (f32[32,1024]{1,0:T(8,128)S(1)}, f32[32,1024]{1,0:T(8,128)S(1)}, u32[]{:S(2)}, u32[]{:S(2)}) collective-permute-start(f32[32,1024]{1,0:T(8,128)S(1)} %shard_map.39), channel_id=1, source_target_pairs={{16,32},{48,64},{80,96},{112,128},{144,160},{176,192},{208,224},{2... | collective-permute-start | bytes 393224 | tf_op jit(solution)/shard_map/ppermute | solution.py:109
  52.8 1.0 %shard_map.38 = (f32[32,1024]{1,0:T(8,128)S(1)}, f32[32,1024]{1,0:T(8,128)S(1)}) custom-call(s32[1]{0:T(128)} %bitcast.odd_ref, bf16[512,1024]{1,0:T(8,128)(2,1)S(1)} %bitcast.6, bf16[27,32,512]{2,1,0:T(8,128)(2,1)S(1)} %copy-done), custom_call_target="tpu_custom_call" | custom-call | tf_op jit(solution)/shard_map/pallas_call | solution.py:77
  53.8 3.5 %collective-permute-start.1 = (f32[32,1024]{1,0:T(8,128)S(1)}, f32[32,1024]{1,0:T(8,128)S(1)}, u32[]{:S(2)}, u32[]{:S(2)}) collective-permute-start(f32[32,1024]{1,0:T(8,128)S(1)} %get-tuple-element.8), channel_id=1, source_target_pairs={{0,16},{16,0},{32,48},{48,32},{64,80},{80,64},{96,112},{112,96},{1... | collective-permute-start | bytes 393224 | tf_op jit(solution)/shard_map/ppermute | solution.py:111
  57.3 1.9 %collective-permute-done.second_ref = f32[32,1024]{1,0:T(8,128)S(1)} collective-permute-done((f32[32,1024]{1,0:T(8,128)S(1)}, f32[32,1024]{1,0:T(8,128)S(1)}, u32[]{:S(2)}, u32[]{:S(2)}) %collective-permute-start) | collective-permute-done | bytes 131104 | tf_op jit(solution)/shard_map/ppermute | solution.py:109
  59.3 0.0 copy-start.2
  59.3 0.0 collective-permute-done.1
  59.3 0.6 %copy-done.2 = f32[32]{0:T(128)S(1)} copy-done((f32[32]{0:T(128)S(1)}, f32[32]{0:T(128)}, u32[]{:S(2)}) %copy-start.2) | copy-done | bytes 152
  59.9 0.7 %fusion = bf16[32,1,1024]{2,0,1:T(8,128)(2,1)} fusion(f32[32,1024]{1,0:T(8,128)S(1)} %shard_map.40, f32[32,1024]{1,0:T(8,128)S(1)} %collective-permute-done.1, f32[32]{0:T(128)S(1)} %copy-done.2), kind=kLoop, calls=%fused_computation.1 | loop fusion | flops 98304 | bytes 327808 | tf_op jit(solution)/shard_map/convert_element_type | solution.py:113
  (1 shorter events, 0.0 us)
Async XLA Ops:
  0.0 0.8 %copy-start.1 = (bf16[32,1,1024]{2,0,1:T(8,128)(2,1)S(1)}, bf16[32,1,1024]{2,0,1:T(8,128)(2,1)}, u32[]{:S(2)}) copy-start(bf16[32,1,1024]{2,0,1:T(8,128)(2,1)} %param.3) | copy-start | bytes 196612
  1.9 48.3 %copy-start = (bf16[27,32,512]{2,1,0:T(8,128)(2,1)S(1)}, bf16[27,32,512]{2,1,0:T(8,128)(2,1)}, u32[]{:S(2)}) copy-start(bf16[27,32,512]{2,1,0:T(8,128)(2,1)} %weight_ref.3) | copy-start | bytes 2654212
  1.9 48.3 %all-to-all-start = ((bf16[16,32,1024]{2,1,0:T(8,128)(2,1)}), bf16[16,32,1024]{2,1,0:T(8,128)(2,1)S(1)}, u32[]{:S(2)}, u32[]{:S(2)}) async-start(bf16[16,32,1024]{2,1,0:T(8,128)(2,1)} %shard_map.37), calls=%async_computation | async-start | bytes 2097152 | tf_op jit(solution)/shard_map/all_to_all | solution.py:102
  50.9 8.4 %collective-permute-start = (f32[32,1024]{1,0:T(8,128)S(1)}, f32[32,1024]{1,0:T(8,128)S(1)}, u32[]{:S(2)}, u32[]{:S(2)}) collective-permute-start(f32[32,1024]{1,0:T(8,128)S(1)} %shard_map.39), channel_id=1, source_target_pairs={{16,32},{48,64},{80,96},{112,128},{144,160},{176,192},{208,224},{2... | collective-permute-start | bytes 393224 | tf_op jit(solution)/shard_map/ppermute | solution.py:109
  53.8 5.5 %collective-permute-start.1 = (f32[32,1024]{1,0:T(8,128)S(1)}, f32[32,1024]{1,0:T(8,128)S(1)}, u32[]{:S(2)}, u32[]{:S(2)}) collective-permute-start(f32[32,1024]{1,0:T(8,128)S(1)} %get-tuple-element.8), channel_id=1, source_target_pairs={{0,16},{16,0},{32,48},{48,32},{64,80},{80,64},{96,112},{112,96},{1... | collective-permute-start | bytes 393224 | tf_op jit(solution)/shard_map/ppermute | solution.py:111
  59.3 0.7 %copy-start.2 = (f32[32]{0:T(128)S(1)}, f32[32]{0:T(128)}, u32[]{:S(2)}) copy-start(f32[32]{0:T(128)} %param.5) | copy-start | bytes 388

commit v3 on v2

v3 whole, which is shorter than its diff:
```python
import functools

import jax
import jax.numpy as jnp
from jax import lax
from jax.experimental import pallas as pl
from jax.experimental.pallas import tpu as pltpu
from jax.sharding import PartitionSpec as P

SIDE = 32


def shifted_rows(value, rows):
    cells = value.shape[1]
    place = lax.broadcasted_iota(jnp.int32, value.shape, 1)
    moved = pltpu.roll(value, (rows * SIDE) % cells, 1)
    inside = place >= rows * SIDE if rows > 0 else place < cells + rows * SIDE
    return jnp.where(inside, moved, 0.0)


def shifted_cols(value, cols):
    cells = value.shape[1]
    column = lax.broadcasted_iota(jnp.int32, value.shape, 1) % SIDE
    moved = pltpu.roll(value, cols % cells, 1)
    inside = column >= 1 if cols > 0 else column <= SIDE - 2
    return jnp.where(inside, moved, 0.0)


VMEM = pl.BlockSpec(memory_space=pltpu.VMEM)
SMEM = pl.BlockSpec(memory_space=pltpu.SMEM)
PARAMS = pltpu.CompilerParams(vmem_limit_bytes=40 * 1024 * 1024)


def pick_kernel(block, place_ref, weight_ref, own_ref, send_ref):
    taps, out_rows, channels = weight_ref.shape
    rows = weight_ref[...].reshape(taps * out_rows, channels)
    shape = (channels, channels // 2)
    source = lax.broadcasted_iota(jnp.int32, shape, 0)
    target = lax.broadcasted_iota(jnp.int32, shape, 1)
    side = target // block % 2
    member = target // (2 * block)
    base = side * (channels // 2) + 2 * member * block + target % block
    for ref, parity in ((send_ref, 1 - place_ref[1]), (own_ref, place_ref[1])):
        matrix = jnp.where(source == base + parity * block, 1.0, 0.0).astype(jnp.bfloat16)
        picked = jnp.dot(rows, matrix, preferred_element_type=jnp.float32)
        ref[...] = picked.astype(jnp.bfloat16)


def picked(block, place, weights):
    taps, out_rows, channels = weights.shape
    out = jax.ShapeDtypeStruct((taps * out_rows, channels // 2), weights.dtype)
    return pl.pallas_call(
        functools.partial(pick_kernel, block),
        out_shape=(out, out),
        in_specs=[SMEM, VMEM],
        out_specs=(VMEM, VMEM),
        compiler_params=PARAMS,
    )(place, weights)


def add_kernel(first_ref, second_ref, out_ref):
    out_ref[...] = first_ref[...] + second_ref[...]


def added(first, second):
    return pl.pallas_call(
        add_kernel,
        out_shape=jax.ShapeDtypeStruct(first.shape, first.dtype),
        in_specs=[VMEM, VMEM],
        out_specs=VMEM,
        compiler_params=PARAMS,
        cost_estimate=pl.CostEstimate(flops=10**10, bytes_accessed=0, transcendentals=0),
    )(first, second)


def in_plane(product):
    rows = product.shape[0] // 9
    taps = [product[tap * rows : (tap + 1) * rows] for tap in range(9)]
    by_col = [
        taps[3 + col] + shifted_rows(taps[col], 1) + shifted_rows(taps[6 + col], -1)
        for col in range(3)
    ]
    return by_col[1] + shifted_cols(by_col[0], 1) + shifted_cols(by_col[2], -1)


def plane_taps(plane, weight_ref, plane_off):
    rows = weight_ref.shape[0] // 3
    group = weight_ref[pl.ds(plane_off * rows, rows), :]
    return in_plane(jnp.dot(group, plane, preferred_element_type=jnp.float32))


def next_kernel(place_ref, plane_ref, own_ref, other_ref, next_ref):
    plane = plane_ref[...]
    away = 2 - 2 * place_ref[0]
    out_rows = next_ref.shape[0] // 2
    next_ref[:out_rows] = plane_taps(plane, own_ref, away)
    next_ref[out_rows:] = plane_taps(plane, other_ref, away)


def rest_kernel(place_ref, plane_ref, own_ref, other_ref, pair_ref, centre_ref):
    plane = plane_ref[...]
    out_rows = pair_ref.shape[0] // 2
    for ref, off in ((pair_ref, 2 * place_ref[0]), (centre_ref, 1)):
        ref[:out_rows] = plane_taps(plane, own_ref, off)
        ref[out_rows:] = plane_taps(plane, other_ref, off)


def taps(body, outs, place, plane, own, other):
    out_rows = 2 * own.shape[0] // 27
    out = jax.ShapeDtypeStruct((out_rows, plane.shape[1]), jnp.float32)
    return pl.pallas_call(
        body,
        out_shape=(out,) * outs,
        in_specs=[SMEM] + [VMEM] * 3,
        out_specs=(VMEM,) * outs,
        compiler_params=PARAMS,
    )(place, plane, own, other)


def on_device(volume, kernel, channel_bias):
    own_in, planes, cells = volume.shape
    own_out = kernel.shape[1]
    filt = lax.axis_size("filt")
    slabs = lax.axis_size("slab")
    ring = filt // 2
    rings = [[i, i + ring] for i in range(ring)]
    partners = [(i, i ^ 1) for i in range(filt)]
    alike = [
        list(range(half * ring + parity, (half + 1) * ring, 2))
        for half in range(2)
        for parity in range(2)
    ]
    pairs = [(i, i ^ 1) for i in range(slabs)]
    nexts = [(i, i + 1) for i in range(1, slabs - 1, 2)]
    nexts += [(target, source) for source, target in nexts]
    place = jnp.stack([lax.axis_index("slab") % 2, lax.axis_index("filt") % 2])
    place = place.astype(jnp.int32)

    own, for_partner = picked(own_in, place, kernel)
    other = lax.ppermute(for_partner, "filt", partners)
    block = volume.reshape(own_in, cells)
    both = lax.all_gather(block, "filt", axis=0, tiled=True, axis_index_groups=rings)
    plane = lax.all_gather(both, "filt", axis=0, tiled=True, axis_index_groups=alike)

    (to_next,) = taps(next_kernel, 1, place, plane, own, other)
    from_next = lax.ppermute(to_next, "slab", nexts)
    to_pair, centre = taps(rest_kernel, 2, place, plane, own, other)
    from_pair = lax.ppermute(to_pair, "slab", pairs)
    centre = added(centre, from_next)
    from_other = lax.ppermute(centre[own_out:] + from_pair[own_out:], "filt", partners)
    summed = centre[:own_out] + from_pair[:own_out] + from_other + channel_bias[:, None]
    return summed.reshape(own_out, planes, cells).astype(jnp.bfloat16)


def solution(mesh):
    return jax.shard_map(
        on_device,
        mesh=mesh,
        in_specs=(P("filt", "slab", None), P(None, "filt", None), P("filt")),
        out_specs=P("filt", "slab", None),
        check_vma=False,
    )
```

time: 60.9 us -> 57.4 us (0.943)
  the two profiles are of different devices: /device:TPU:8 before, /device:TPU:56 now
where the time goes in v3:
time: 57.4 us; the launch traced here: 57.2 us
  blocking collectives  31.6 us (55%)
  starting transfers between devices  11.6 us (20%)
  waiting for transfers between devices  7.31 us (13%)
  Pallas kernels  4.59 us (8%)
  local copies, waits for them, and re-layouts  1.18 us (2%)
  other arithmetic  0.8 us (1%)
    all_gather x1, blocking collectives, on_device(): lax.all_gather(both, 'filt', axis=0, tiled=True, axis_index_groups=alike)  22.1 us
    all_gather x1, blocking collectives, on_device(): lax.all_gather(block, 'filt', axis=0, tiled=True, axis_index_groups=rings)  9.55 us
    ppermute x1, waiting for transfers between devices, on_device(): lax.ppermute(centre[own_out:] + from_pair[own_out:], 'filt', partners)  4.93 us
    ppermute x1, starting transfers between devices, on_device(): other = lax.ppermute(for_partner, 'filt', partners)  4.28 us
    ppermute x1, starting transfers between devices, on_device(): from_pair = lax.ppermute(to_pair, 'slab', pairs)  3.5 us
    pallas_call x2, Pallas kernels, taps(): pl.pallas_call(body, out_shape=(out,) * outs, in_specs=[SMEM] + [VMEM] *...  3.35 us
    ppermute x1, waiting for transfers between devices, on_device(): from_next = lax.ppermute(to_next, 'slab', nexts)  2.37 us
    ppermute x1, starting transfers between devices, on_device(): from_next = lax.ppermute(to_next, 'slab', nexts)  1.92 us
  transfers between devices with their start and end apart: 4, of which 2 were waited for; matrix products, arithmetic and copies ran while one was open for 0% of the time, Pallas kernels for 4%

profile of v3, /device:TPU:56, one launch (start us, length us, event | category | flops | bytes accessed | tf_op | source)
XLA Modules:
  0.0 57.2 jit_solution(7861806496400472425)
XLA Ops:
  0.0 0.1 pad_add_fusion.place_ref
  0.1 0.0 copy-start
  0.1 1.2 %copy-done = bf16[27,32,512]{2,1,0:T(8,128)(2,1)S(1)} copy-done((bf16[27,32,512]{2,1,0:T(8,128)(2,1)S(1)}, bf16[27,32,512]{2,1,0:T(8,128)(2,1)}, u32[]{:S(2)}) %copy-start) | copy-done | bytes 884760
  1.2 0.0 copy-start.1
  1.2 1.2 %shard_map.37 = (bf16[864,256]{1,0:T(8,128)(2,1)S(1)}, bf16[864,256]{1,0:T(8,128)(2,1)S(1)}) custom-call(s32[2]{0:T(128)S(1)} %pad_add_fusion.place_ref, bf16[27,32,512]{2,1,0:T(8,128)(2,1)S(1)} %copy-done), custom_call_target="tpu_custom_call" | custom-call | tf_op jit(solution)/shard_map/pallas_call | solution.py:52
  2.5 4.3 %collective-permute-start = (bf16[864,256]{1,0:T(8,128)(2,1)S(1)}, bf16[864,256]{1,0:T(8,128)(2,1)S(1)}, u32[]{:S(2)}, u32[]{:S(2)}) collective-permute-start(bf16[864,256]{1,0:T(8,128)(2,1)S(1)} %get-tuple-element.10), channel_id=1, source_target_pairs={{0,1},{1,0},{2,3},{3,2},{4,5},{5,4},{6,7},{7,6},{8,9},{9,8},{10,11... | collective-permute-start | bytes 1327112 | tf_op jit(solution)/shard_map/ppermute | solution.py:140
  6.7 0.0 copy-done.1
  6.8 9.6 %all-gather = bf16[64,1,1024]{2,0,1:T(8,128)(2,1)S(1)} all-gather(bf16[32,1,1024]{2,0,1:T(8,128)(2,1)S(1)} %copy-done.1), channel_id=2, replica_groups={{0,8},{1,9},{2,10},{3,11},{4,12},{5,13},{6,14},{7,15},{16,24},{17,25},{..., dimensions={0}, use_global_device_ids=true | all-gather | bytes 196608 | tf_op jit(solution)/shard_map/all_gather | solution.py:142
  16.3 22.1 %all-gather.1 = bf16[256,1,1024]{2,0,1:T(8,128)(2,1)S(1)} all-gather(bf16[64,1,1024]{2,0,1:T(8,128)(2,1)S(1)} %all-gather), channel_id=3, replica_groups={{0,2,4,6},{1,3,5,7},{8,10,12,14},{9,11,13,15},{16,18,20,22},{17,19,21,2..., dimensions={0}, use_global_device_ids=true | all-gather | bytes 655360 | tf_op jit(solution)/shard_map/all_gather | solution.py:143
  38.4 0.0 collective-permute-done.other_ref
  38.4 1.4 %shard_map.39 = f32[64,1024]{1,0:T(8,128)S(1)} custom-call(s32[2]{0:T(128)S(1)} %pad_add_fusion.place_ref, bf16[256,1024]{1,0:T(8,128)(2,1)S(1)} %bitcast.5, bf16[864,256]{1,0:T(8,128)(2,1)S(1)} %get-tuple-element.9.own_ref, bf16[864,256]{1,0:T(8,128)(2,1)S(1)} %collective-permute-done.other_ref), custom_call_target="tpu_custom_call" | custom-call | tf_op jit(solution)/shard_map/pallas_call | solution.py:111
  39.7 1.9 %collective-permute-start.1 = (f32[64,1024]{1,0:T(8,128)S(1)}, f32[64,1024]{1,0:T(8,128)S(1)}, u32[]{:S(2)}, u32[]{:S(2)}) collective-permute-start(f32[64,1024]{1,0:T(8,128)S(1)} %shard_map.39), channel_id=1, source_target_pairs={{16,32},{48,64},{80,96},{112,128},{144,160},{176,192},{208,224},{2... | collective-permute-start | bytes 786440 | tf_op jit(solution)/shard_map/ppermute | solution.py:146
  41.7 2.0 %shard_map.38 = (f32[64,1024]{1,0:T(8,128)S(1)}, f32[64,1024]{1,0:T(8,128)S(1)}) custom-call(s32[2]{0:T(128)S(1)} %pad_add_fusion.place_ref, bf16[256,1024]{1,0:T(8,128)(2,1)S(1)} %bitcast.6, bf16[864,256]{1,0:T(8,128)(2,1)S(1)} %get-tuple-element.9.own_ref, bf16[864,256]{1,0:T(8,128)(2,1)S(1)} %collective-permute-done.other_ref), custom_call_target="tpu_custom_call" | custom-call | tf_op jit(solution)/shard_map/pallas_call | solution.py:111
  43.7 3.5 %collective-permute-start.2 = (f32[64,1024]{1,0:T(8,128)S(1)}, f32[64,1024]{1,0:T(8,128)S(1)}, u32[]{:S(2)}, u32[]{:S(2)}) collective-permute-start(f32[64,1024]{1,0:T(8,128)S(1)} %get-tuple-element.12), channel_id=1, source_target_pairs={{0,16},{16,0},{32,48},{48,32},{64,80},{80,64},{96,112},{112,96},{1... | collective-permute-start | bytes 786440 | tf_op jit(solution)/shard_map/ppermute | solution.py:148
  47.2 2.4 %collective-permute-done.1.second_ref = f32[64,1024]{1,0:T(8,128)S(1)} collective-permute-done((f32[64,1024]{1,0:T(8,128)S(1)}, f32[64,1024]{1,0:T(8,128)S(1)}, u32[]{:S(2)}, u32[]{:S(2)}) %collective-permute-start.1) | collective-permute-done | bytes 262176 | tf_op jit(solution)/shard_map/ppermute | solution.py:146
  49.6 0.0 copy-start.2
  49.6 0.0 collective-permute-done.2
  49.6 1.9 %collective-permute-start.3 = (f32[32,1024]{1,0:T(8,128)S(1)}, f32[32,1024]{1,0:T(8,128)S(1)}, u32[]{:S(2)}, u32[]{:S(2)}) collective-permute-start(f32[32,1024]{1,0:T(8,128)S(1)} %slice_add_fusion), channel_id=1, source_target_pairs={{0,1},{1,0},{2,3},{3,2},{4,5},{5,4},{6,7},{7,6},{8,9},{9,8},{10,11... | collective-permute-start | bytes 393224 | tf_op jit(solution)/shard_map/ppermute | solution.py:150
  51.6 4.9 %collective-permute-done.3 = f32[32,1024]{1,0:T(8,128)S(1)} collective-permute-done((f32[32,1024]{1,0:T(8,128)S(1)}, f32[32,1024]{1,0:T(8,128)S(1)}, u32[]{:S(2)}, u32[]{:S(2)}) %collective-permute-start.3) | collective-permute-done | bytes 131104 | tf_op jit(solution)/shard_map/ppermute | solution.py:150
  56.5 0.0 copy-done.2
  56.5 0.7 %fusion.3 = bf16[32,1,1024]{2,0,1:T(8,128)(2,1)} fusion(f32[32,1024]{1,0:T(8,128)S(1)} %collective-permute-done.3, f32[64,1024]{1,0:T(8,128)S(1)} %collective-permute-done.2, f32[64,1024]{1,0:T(8,128)S(1)} %shard_map.40, f32[32]{0:T(128)S(1)} %copy-done.2), kind=kLoop, calls=%fused_computation.5 | loop fusion | flops 131072 | bytes 458880 | tf_op jit(solution)/shard_map/convert_element_type | solution.py:152
  (2 shorter events, 0.1 us)
Async XLA Ops:
  0.1 1.2 %copy-start = (bf16[27,32,512]{2,1,0:T(8,128)(2,1)S(1)}, bf16[27,32,512]{2,1,0:T(8,128)(2,1)}, u32[]{:S(2)}) copy-start(bf16[27,32,512]{2,1,0:T(8,128)(2,1)} %weight_ref.1) | copy-start | bytes 2654212
  1.2 5.5 %copy-start.1 = (bf16[32,1,1024]{2,0,1:T(8,128)(2,1)S(1)}, bf16[32,1,1024]{2,0,1:T(8,128)(2,1)}, u32[]{:S(2)}) copy-start(bf16[32,1,1024]{2,0,1:T(8,128)(2,1)} %param.3) | copy-start | bytes 196612
  2.5 35.9 %collective-permute-start = (bf16[864,256]{1,0:T(8,128)(2,1)S(1)}, bf16[864,256]{1,0:T(8,128)(2,1)S(1)}, u32[]{:S(2)}, u32[]{:S(2)}) collective-permute-start(bf16[864,256]{1,0:T(8,128)(2,1)S(1)} %get-tuple-element.10), channel_id=1, source_target_pairs={{0,1},{1,0},{2,3},{3,2},{4,5},{5,4},{6,7},{7,6},{8,9},{9,8},{10,11... | collective-permute-start | bytes 1327112 | tf_op jit(solution)/shard_map/ppermute | solution.py:140
  39.7 9.8 %collective-permute-start.1 = (f32[64,1024]{1,0:T(8,128)S(1)}, f32[64,1024]{1,0:T(8,128)S(1)}, u32[]{:S(2)}, u32[]{:S(2)}) collective-permute-start(f32[64,1024]{1,0:T(8,128)S(1)} %shard_map.39), channel_id=1, source_target_pairs={{16,32},{48,64},{80,96},{112,128},{144,160},{176,192},{208,224},{2... | collective-permute-start | bytes 786440 | tf_op jit(solution)/shard_map/ppermute | solution.py:146
  43.7 5.9 %collective-permute-start.2 = (f32[64,1024]{1,0:T(8,128)S(1)}, f32[64,1024]{1,0:T(8,128)S(1)}, u32[]{:S(2)}, u32[]{:S(2)}) collective-permute-start(f32[64,1024]{1,0:T(8,128)S(1)} %get-tuple-element.12), channel_id=1, source_target_pairs={{0,16},{16,0},{32,48},{48,32},{64,80},{80,64},{96,112},{112,96},{1... | collective-permute-start | bytes 786440 | tf_op jit(solution)/shard_map/ppermute | solution.py:148
  49.6 6.9 %copy-start.2 = (f32[32]{0:T(128)S(1)}, f32[32]{0:T(128)}, u32[]{:S(2)}) copy-start(f32[32]{0:T(128)} %param.5) | copy-start | bytes 388
  49.6 6.9 %collective-permute-start.3 = (f32[32,1024]{1,0:T(8,128)S(1)}, f32[32,1024]{1,0:T(8,128)S(1)}, u32[]{:S(2)}, u32[]{:S(2)}) collective-permute-start(f32[32,1024]{1,0:T(8,128)S(1)} %slice_add_fusion), channel_id=1, source_target_pairs={{0,1},{1,0},{2,3},{3,2},{4,5},{5,4},{6,7},{7,6},{8,9},{9,8},{10,11... | collective-permute-start | bytes 393224 | tf_op jit(solution)/shard_map/ppermute | solution.py:150

commit v4 on v3

v4 whole, which is shorter than its diff:
```python
import functools

import jax
import jax.numpy as jnp
from jax import lax
from jax.experimental import pallas as pl
from jax.experimental.pallas import tpu as pltpu
from jax.sharding import PartitionSpec as P

SIDE = 32


def shifted_rows(value, rows):
    cells = value.shape[1]
    place = lax.broadcasted_iota(jnp.int32, value.shape, 1)
    moved = pltpu.roll(value, (rows * SIDE) % cells, 1)
    inside = place >= rows * SIDE if rows > 0 else place < cells + rows * SIDE
    return jnp.where(inside, moved, 0.0)


def shifted_cols(value, cols):
    cells = value.shape[1]
    column = lax.broadcasted_iota(jnp.int32, value.shape, 1) % SIDE
    moved = pltpu.roll(value, cols % cells, 1)
    inside = column >= 1 if cols > 0 else column <= SIDE - 2
    return jnp.where(inside, moved, 0.0)


VMEM = pl.BlockSpec(memory_space=pltpu.VMEM)
SMEM = pl.BlockSpec(memory_space=pltpu.SMEM)
PARAMS = pltpu.CompilerParams(vmem_limit_bytes=40 * 1024 * 1024)


def add_kernel(first_ref, second_ref, out_ref):
    out_ref[...] = first_ref[...] + second_ref[...]


def added(first, second):
    return pl.pallas_call(
        add_kernel,
        out_shape=jax.ShapeDtypeStruct(first.shape, first.dtype),
        in_specs=[VMEM, VMEM],
        out_specs=VMEM,
        compiler_params=PARAMS,
        cost_estimate=pl.CostEstimate(flops=10**10, bytes_accessed=0, transcendentals=0),
    )(first, second)


def in_plane(product):
    rows = product.shape[0] // 9
    taps = [product[tap * rows : (tap + 1) * rows] for tap in range(9)]
    by_col = [
        taps[3 + col] + shifted_rows(taps[col], 1) + shifted_rows(taps[6 + col], -1)
        for col in range(3)
    ]
    return by_col[1] + shifted_cols(by_col[0], 1) + shifted_cols(by_col[2], -1)


def plane_taps(plane, weight_ref, plane_off):
    out_rows, channels = weight_ref.shape[1:]
    group = weight_ref[pl.ds(9 * plane_off, 9)].reshape(9 * out_rows, channels)
    return in_plane(jnp.dot(group, plane, preferred_element_type=jnp.float32))


def next_kernel(block, place_ref, own_ref, low_ref, high_ref, weight_ref, next_ref, plane_ref):
    parity = place_ref[1]
    sides = 2
    members = own_ref.shape[0] // (sides * block)
    for member in range(members):
        for side in range(sides):
            row = (sides * member + side) * block
            for ref, first, at in (
                (own_ref, row, parity),
                (low_ref, row, 1 - parity),
                (high_ref, row - low_ref.shape[0], 1 - parity),
            ):
                if 0 <= first < ref.shape[0]:
                    target = (side * 2 * members + 2 * member + at) * block
                    plane_ref[pl.ds(pl.multiple_of(target, block), block)] = ref[
                        first : first + block
                    ]
    next_ref[...] = plane_taps(plane_ref[...], weight_ref, 2 - 2 * place_ref[0])


def rest_kernel(place_ref, plane_ref, weight_ref, pair_ref, centre_ref):
    plane = plane_ref[...]
    pair_ref[...] = plane_taps(plane, weight_ref, 2 * place_ref[0])
    centre_ref[...] = plane_taps(plane, weight_ref, 1)


def called(body, out_shape, *args):
    return pl.pallas_call(
        body,
        out_shape=out_shape,
        in_specs=[SMEM] + [VMEM] * (len(args) - 1),
        out_specs=(VMEM,) * len(out_shape),
        compiler_params=PARAMS,
    )(*args)


def on_device(volume, kernel, channel_bias):
    own_in, planes, cells = volume.shape
    own_out = kernel.shape[1]
    filt = lax.axis_size("filt")
    slabs = lax.axis_size("slab")
    ring = filt // 2
    rings = [[i, i + ring] for i in range(ring)]
    alike = [
        list(range(half * ring + parity, (half + 1) * ring, 2))
        for half in range(2)
        for parity in range(2)
    ]
    down = [(i, i // ring * ring + (i - 1) % ring) for i in range(filt)]
    up = [(target, source) for source, target in down]
    pairs = [(i, i ^ 1) for i in range(slabs)]
    nexts = [(i, i + 1) for i in range(1, slabs - 1, 2)]
    nexts += [(target, source) for source, target in nexts]
    place = jnp.stack([lax.axis_index("slab") % 2, lax.axis_index("filt") % 2])
    place = place.astype(jnp.int32)

    block = volume.reshape(own_in, cells)
    both = lax.all_gather(block, "filt", axis=0, tiled=True, axis_index_groups=rings)
    own = lax.all_gather(both, "filt", axis=0, tiled=True, axis_index_groups=alike)
    half = own.shape[0] // 2
    low = lax.ppermute(own[:half], "filt", down)
    high = lax.ppermute(own[half:], "filt", up)

    part = jax.ShapeDtypeStruct((own_out, cells), jnp.float32)
    whole = jax.ShapeDtypeStruct((filt * own_in, cells), volume.dtype)
    to_next, plane = called(
        functools.partial(next_kernel, own_in), (part, whole), place, own, low, high, kernel
    )
    from_next = lax.ppermute(to_next, "slab", nexts)
    to_pair, centre = called(rest_kernel, (part, part), place, plane, kernel)
    from_pair = lax.ppermute(to_pair, "slab", pairs)
    summed = added(centre, from_next) + from_pair + channel_bias[:, None]
    return summed.reshape(own_out, planes, cells).astype(jnp.bfloat16)


def solution(mesh):
    return jax.shard_map(
        on_device,
        mesh=mesh,
        in_specs=(P("filt", "slab", None), P(None, "filt", None), P("filt")),
        out_specs=P("filt", "slab", None),
        check_vma=False,
    )
```

time: 57.4 us -> 56.3 us (0.981)
  the two profiles are of different devices: /device:TPU:56 before, /device:TPU:16 now
where the time goes in v4:
time: 56.3 us; the launch traced here: 56 us
  blocking collectives  31.9 us (57%)
  starting transfers between devices  13.9 us (25%)
  waiting for transfers between devices  5.85 us (10%)
  Pallas kernels  2.86 us (5%)
  other arithmetic  0.78 us (1%)
  local copies, waits for them, and re-layouts  0.66 us (1%)
    all_gather x1, blocking collectives, on_device(): lax.all_gather(both, 'filt', axis=0, tiled=True, axis_index_groups=alike)  22.5 us
    all_gather x1, blocking collectives, on_device(): lax.all_gather(block, 'filt', axis=0, tiled=True, axis_index_groups=rings)  9.41 us
    ppermute x1, starting transfers between devices, on_device(): low = lax.ppermute(own[:half], 'filt', down)  4.9 us
    ppermute x1, starting transfers between devices, on_device(): high = lax.ppermute(own[half:], 'filt', up)  3.56 us
    ppermute x1, starting transfers between devices, on_device(): from_pair = lax.ppermute(to_pair, 'slab', pairs)  3.5 us
    pallas_call x2, Pallas kernels, called(): pl.pallas_call(body, out_shape=out_shape, in_specs=[SMEM] + [VMEM] * (len...  2.84 us
    ppermute x1, waiting for transfers between devices, on_device(): high = lax.ppermute(own[half:], 'filt', up)  2.31 us
    ppermute x1, waiting for transfers between devices, on_device(): low = lax.ppermute(own[:half], 'filt', down)  2.14 us
  transfers between devices with their start and end apart: 4, of which 3 were waited for; matrix products, arithmetic and copies ran while one was open for 0% of the time, Pallas kernels for 3%

profile of v4, /device:TPU:16, one launch (start us, length us, event | category | flops | bytes accessed | tf_op | source)
XLA Modules:
  0.0 56.0 jit_solution(10139836620303179682)
XLA Ops:
  0.0 9.4 %all-gather = bf16[64,1,1024]{2,0,1:T(8,128)(2,1)S(1)} all-gather(bf16[32,1,1024]{2,0,1:T(8,128)(2,1)} %param.3), channel_id=2, replica_groups={{0,8},{1,9},{2,10},{3,11},{4,12},{5,13},{6,14},{7,15},{16,24},{17,25},{..., dimensions={0}, use_global_device_ids=true | all-gather | bytes 196608 | tf_op jit(solution)/shard_map/all_gather | solution.py:122
  9.4 0.0 copy-start
  9.4 22.5 %all-gather.1 = bf16[256,1,1024]{2,0,1:T(8,128)(2,1)S(1)} all-gather(bf16[64,1,1024]{2,0,1:T(8,128)(2,1)S(1)} %all-gather), channel_id=3, replica_groups={{0,2,4,6},{1,3,5,7},{8,10,12,14},{9,11,13,15},{16,18,20,22},{17,19,21,2..., dimensions={0}, use_global_device_ids=true | all-gather | bytes 655360 | tf_op jit(solution)/shard_map/all_gather | solution.py:123
  31.9 3.6 %collective-permute-start.1 = (bf16[128,1024]{1,0:T(8,128)(2,1)S(1)}, bf16[128,1024]{1,0:T(8,128)(2,1)S(1)}, u32[]{:S(2)}, u32[]{:S(2)}) collective-permute-start(bf16[128,1024]{1,0:T(8,128)(2,1)S(1)} %get-tuple-element.13), channel_id=1, source_target_pairs={{7,0},{0,1},{1,2},{2,3},{3,4},{4,5},{5,6},{6,7},{15,8},{8,9},{9,10... | collective-permute-start | bytes 786440 | tf_op jit(solution)/shard_map/ppermute | solution.py:126
  35.5 4.9 %collective-permute-start = (bf16[128,1024]{1,0:T(8,128)(2,1)S(1)}, bf16[128,1024]{1,0:T(8,128)(2,1)S(1)}, u32[]{:S(2)}, u32[]{:S(2)}) collective-permute-start(bf16[128,1024]{1,0:T(8,128)(2,1)S(1)} %get-tuple-element.14), channel_id=1, source_target_pairs={{0,7},{1,0},{2,1},{3,2},{4,3},{5,4},{6,5},{7,6},{8,15},{9,8},{10,9... | collective-permute-start | bytes 786440 | tf_op jit(solution)/shard_map/ppermute | solution.py:125
  40.4 0.1 pad_add_fusion.place_ref
  40.5 2.3 %collective-permute-done.1.high_ref = bf16[128,1024]{1,0:T(8,128)(2,1)S(1)} collective-permute-done((bf16[128,1024]{1,0:T(8,128)(2,1)S(1)}, bf16[128,1024]{1,0:T(8,128)(2,1)S(1)}, u32[]{:S(2)}, u32[]{:S(2)}) %collective-permute-start.1) | collective-permute-done | bytes 262176 | tf_op jit(solution)/shard_map/ppermute | solution.py:126
  42.8 2.1 %collective-permute-done.low_ref = bf16[128,1024]{1,0:T(8,128)(2,1)S(1)} collective-permute-done((bf16[128,1024]{1,0:T(8,128)(2,1)S(1)}, bf16[128,1024]{1,0:T(8,128)(2,1)S(1)}, u32[]{:S(2)}, u32[]{:S(2)}) %collective-permute-start) | collective-permute-done | bytes 262176 | tf_op jit(solution)/shard_map/ppermute | solution.py:125
  45.0 0.0 copy-done
  45.0 1.3 %shard_map.37 = (f32[32,1024]{1,0:T(8,128)S(1)}, bf16[512,1024]{1,0:T(8,128)(2,1)S(1)}) custom-call(s32[2]{0:T(128)S(1)} %pad_add_fusion.place_ref, bf16[256,1024]{1,0:T(8,128)(2,1)S(1)} %bitcast.9, bf16[128,1024]{1,0:T(8,128)(2,1)S(1)} %collective-permute-done.low_ref, bf16[128,1024]{1,0:T(8,128)(2,1)S(1)} %collective-permute-done.1.high_ref, ...), custom_call_target="tpu_custom_call" | custom-call | tf_op jit(solution)/shard_map/pallas_call | solution.py:92
  46.3 1.9 %collective-permute-start.2 = (f32[32,1024]{1,0:T(8,128)S(1)}, f32[32,1024]{1,0:T(8,128)S(1)}, u32[]{:S(2)}, u32[]{:S(2)}) collective-permute-start(f32[32,1024]{1,0:T(8,128)S(1)} %get-tuple-element.11), channel_id=1, source_target_pairs={{16,32},{48,64},{80,96},{112,128},{144,160},{176,192},{208,224},{2... | collective-permute-start | bytes 393224 | tf_op jit(solution)/shard_map/ppermute | solution.py:133
  48.2 1.6 %shard_map.38 = (f32[32,1024]{1,0:T(8,128)S(1)}, f32[32,1024]{1,0:T(8,128)S(1)}) custom-call(s32[2]{0:T(128)S(1)} %pad_add_fusion.place_ref, bf16[512,1024]{1,0:T(8,128)(2,1)S(1)} %get-tuple-element.9.plane_ref, bf16[27,32,512]{2,1,0:T(8,128)(2,1)S(1)} %copy-done), custom_call_target="tpu_custom_call" | custom-call | tf_op jit(solution)/shard_map/pallas_call | solution.py:92
  49.8 3.5 %collective-permute-start.3 = (f32[32,1024]{1,0:T(8,128)S(1)}, f32[32,1024]{1,0:T(8,128)S(1)}, u32[]{:S(2)}, u32[]{:S(2)}) collective-permute-start(f32[32,1024]{1,0:T(8,128)S(1)} %get-tuple-element.12), channel_id=1, source_target_pairs={{0,16},{16,0},{32,48},{48,32},{64,80},{80,64},{96,112},{112,96},{1... | collective-permute-start | bytes 393224 | tf_op jit(solution)/shard_map/ppermute | solution.py:135
  53.3 1.4 %collective-permute-done.2.second_ref = f32[32,1024]{1,0:T(8,128)S(1)} collective-permute-done((f32[32,1024]{1,0:T(8,128)S(1)}, f32[32,1024]{1,0:T(8,128)S(1)}, u32[]{:S(2)}, u32[]{:S(2)}) %collective-permute-start.2) | collective-permute-done | bytes 131104 | tf_op jit(solution)/shard_map/ppermute | solution.py:133
  54.7 0.0 copy-start.1
  54.7 0.0 collective-permute-done.3
  54.7 0.6 %copy-done.1 = f32[32]{0:T(128)S(1)} copy-done((f32[32]{0:T(128)S(1)}, f32[32]{0:T(128)}, u32[]{:S(2)}) %copy-start.1) | copy-done | bytes 152
  55.3 0.7 %fusion = bf16[32,1,1024]{2,0,1:T(8,128)(2,1)} fusion(f32[32,1024]{1,0:T(8,128)S(1)} %shard_map.39, f32[32,1024]{1,0:T(8,128)S(1)} %collective-permute-done.3, f32[32]{0:T(128)S(1)} %copy-done.1), kind=kLoop, calls=%fused_computation.3 | loop fusion | flops 98304 | bytes 327808 | tf_op jit(solution)/shard_map/convert_element_type | solution.py:137
  (2 shorter events, 0.1 us)
Async XLA Ops:
  9.4 35.6 %copy-start = (bf16[27,32,512]{2,1,0:T(8,128)(2,1)S(1)}, bf16[27,32,512]{2,1,0:T(8,128)(2,1)}, u32[]{:S(2)}) copy-start(bf16[27,32,512]{2,1,0:T(8,128)(2,1)} %weight_ref.3) | copy-start | bytes 2654212
  31.9 10.9 %collective-permute-start.1 = (bf16[128,1024]{1,0:T(8,128)(2,1)S(1)}, bf16[128,1024]{1,0:T(8,128)(2,1)S(1)}, u32[]{:S(2)}, u32[]{:S(2)}) collective-permute-start(bf16[128,1024]{1,0:T(8,128)(2,1)S(1)} %get-tuple-element.13), channel_id=1, source_target_pairs={{7,0},{0,1},{1,2},{2,3},{3,4},{4,5},{5,6},{6,7},{15,8},{8,9},{9,10... | collective-permute-start | bytes 786440 | tf_op jit(solution)/shard_map/ppermute | solution.py:126
  35.5 9.5 %collective-permute-start = (bf16[128,1024]{1,0:T(8,128)(2,1)S(1)}, bf16[128,1024]{1,0:T(8,128)(2,1)S(1)}, u32[]{:S(2)}, u32[]{:S(2)}) collective-permute-start(bf16[128,1024]{1,0:T(8,128)(2,1)S(1)} %get-tuple-element.14), channel_id=1, source_target_pairs={{0,7},{1,0},{2,1},{3,2},{4,3},{5,4},{6,5},{7,6},{8,15},{9,8},{10,9... | collective-permute-start | bytes 786440 | tf_op jit(solution)/shard_map/ppermute | solution.py:125
  46.3 8.4 %collective-permute-start.2 = (f32[32,1024]{1,0:T(8,128)S(1)}, f32[32,1024]{1,0:T(8,128)S(1)}, u32[]{:S(2)}, u32[]{:S(2)}) collective-permute-start(f32[32,1024]{1,0:T(8,128)S(1)} %get-tuple-element.11), channel_id=1, source_target_pairs={{16,32},{48,64},{80,96},{112,128},{144,160},{176,192},{208,224},{2... | collective-permute-start | bytes 393224 | tf_op jit(solution)/shard_map/ppermute | solution.py:133
  49.8 4.9 %collective-permute-start.3 = (f32[32,1024]{1,0:T(8,128)S(1)}, f32[32,1024]{1,0:T(8,128)S(1)}, u32[]{:S(2)}, u32[]{:S(2)}) collective-permute-start(f32[32,1024]{1,0:T(8,128)S(1)} %get-tuple-element.12), channel_id=1, source_target_pairs={{0,16},{16,0},{32,48},{48,32},{64,80},{80,64},{96,112},{112,96},{1... | collective-permute-start | bytes 393224 | tf_op jit(solution)/shard_map/ppermute | solution.py:135
  54.7 0.7 %copy-start.1 = (f32[32]{0:T(128)S(1)}, f32[32]{0:T(128)}, u32[]{:S(2)}) copy-start(f32[32]{0:T(128)} %param.5) | copy-start | bytes 388

commit v5 on v4

--- a/solution.py
+++ b/solution.py
@@ -62,8 +62,7 @@
     return in_plane(jnp.dot(group, plane, preferred_element_type=jnp.float32))
 
 
-def next_kernel(block, place_ref, own_ref, low_ref, high_ref, weight_ref, next_ref, plane_ref):
-    parity = place_ref[1]
+def in_order(block, parity, own_ref, low_ref, high_ref, plane_ref):
     sides = 2
     members = own_ref.shape[0] // (sides * block)
     for member in range(members):
@@ -79,21 +78,31 @@
                     plane_ref[pl.ds(pl.multiple_of(target, block), block)] = ref[
                         first : first + block
                     ]
-    next_ref[...] = plane_taps(plane_ref[...], weight_ref, 2 - 2 * place_ref[0])
 
 
-def rest_kernel(place_ref, plane_ref, weight_ref, pair_ref, centre_ref):
+def away_kernel(
+    block, place_ref, own_ref, low_ref, high_ref, weight_ref, next_ref, pair_ref, plane_ref
+):
+    in_order(block, place_ref[1], own_ref, low_ref, high_ref, plane_ref)
     plane = plane_ref[...]
+    next_ref[...] = plane_taps(plane, weight_ref, 2 - 2 * place_ref[0])
     pair_ref[...] = plane_taps(plane, weight_ref, 2 * place_ref[0])
-    centre_ref[...] = plane_taps(plane, weight_ref, 1)
 
 
-def called(body, out_shape, *args):
+def centre_kernel(
+    block, place_ref, own_ref, low_ref, high_ref, weight_ref, centre_ref, plane_ref
+):
+    in_order(block, place_ref[1], own_ref, low_ref, high_ref, plane_ref)
+    centre_ref[...] = plane_taps(plane_ref[...], weight_ref, 1)
+
+
+def called(body, out_shape, scratch, *args):
     return pl.pallas_call(
         body,
         out_shape=out_shape,
         in_specs=[SMEM] + [VMEM] * (len(args) - 1),
         out_specs=(VMEM,) * len(out_shape),
+        scratch_shapes=[scratch],
         compiler_params=PARAMS,
     )(*args)
 
@@ -126,13 +135,14 @@
     high = lax.ppermute(own[half:], "filt", up)
 
     part = jax.ShapeDtypeStruct((own_out, cells), jnp.float32)
-    whole = jax.ShapeDtypeStruct((filt * own_in, cells), volume.dtype)
-    to_next, plane = called(
-        functools.partial(next_kernel, own_in), (part, whole), place, own, low, high, kernel
+    scratch = pltpu.VMEM((filt * own_in, cells), volume.dtype)
+    gathered = (place, own, low, high, kernel)
+    to_next, to_pair = called(
+        functools.partial(away_kernel, own_in), (part, part), scratch, *gathered
     )
     from_next = lax.ppermute(to_next, "slab", nexts)
-    to_pair, centre = called(rest_kernel, (part, part), place, plane, kernel)
     from_pair = lax.ppermute(to_pair, "slab", pairs)
+    (centre,) = called(functools.partial(centre_kernel, own_in), (part,), scratch, *gathered)
     summed = added(centre, from_next) + from_pair + channel_bias[:, None]
     return summed.reshape(own_out, planes, cells).astype(jnp.bfloat16)
 

time: 56.3 us -> 56 us (level)
  local copies, waits for them, and re-layouts: 0.66 us -> 0.04 us
    unnamed x4, local copies, waits for them, and re-layouts: 0.63 us -> 0.01 us
  transfers between devices with their start and end apart: 4 -> 4, of which waited for: 3 -> 3; matrix products, arithmetic and copies ran while one was open for 0% -> 0% of each run, Pallas kernels for 3% -> 2%
where the time goes in v5:
time: 56 us; the launch traced here: 55.8 us
  blocking collectives  31.9 us (57%)
  starting transfers between devices  13.9 us (25%)
  waiting for transfers between devices  6.11 us (11%)
  Pallas kernels  2.92 us (5%)
  other arithmetic  0.78 us (1%)
    all_gather x1, blocking collectives, on_device(): lax.all_gather(both, 'filt', axis=0, tiled=True, axis_index_groups=alike)  22.5 us
    all_gather x1, blocking collectives, on_device(): lax.all_gather(block, 'filt', axis=0, tiled=True, axis_index_groups=rings)  9.41 us
    ppermute x1, starting transfers between devices, on_device(): low = lax.ppermute(own[:half], 'filt', down)  4.9 us
    ppermute x1, starting transfers between devices, on_device(): high = lax.ppermute(own[half:], 'filt', up)  3.56 us
    ppermute x1, starting transfers between devices, on_device(): from_pair = lax.ppermute(to_pair, 'slab', pairs)  3.5 us
    pallas_call x2, Pallas kernels, called(): pl.pallas_call(body, out_shape=out_shape, in_specs=[SMEM] + [VMEM] * (len...  2.9 us
    ppermute x1, waiting for transfers between devices, on_device(): high = lax.ppermute(own[half:], 'filt', up)  2.31 us
    ppermute x1, waiting for transfers between devices, on_device(): low = lax.ppermute(own[:half], 'filt', down)  2.14 us
  transfers between devices with their start and end apart: 4, of which 3 were waited for; matrix products, arithmetic and copies ran while one was open for 0% of the time, Pallas kernels for 2%

profile of v5, /device:TPU:16, one launch (start us, length us, event | category | flops | bytes accessed | tf_op | source)
XLA Modules:
  0.0 55.8 jit_solution(3663811016760237620)
XLA Ops:
  0.0 9.4 %all-gather = bf16[64,1,1024]{2,0,1:T(8,128)(2,1)S(1)} all-gather(bf16[32,1,1024]{2,0,1:T(8,128)(2,1)} %param.3), channel_id=2, replica_groups={{0,8},{1,9},{2,10},{3,11},{4,12},{5,13},{6,14},{7,15},{16,24},{17,25},{..., dimensions={0}, use_global_device_ids=true | all-gather | bytes 196608 | tf_op jit(solution)/shard_map/all_gather | solution.py:131
  9.4 0.0 copy-start
  9.4 22.5 %all-gather.1 = bf16[256,1,1024]{2,0,1:T(8,128)(2,1)S(1)} all-gather(bf16[64,1,1024]{2,0,1:T(8,128)(2,1)S(1)} %all-gather), channel_id=3, replica_groups={{0,2,4,6},{1,3,5,7},{8,10,12,14},{9,11,13,15},{16,18,20,22},{17,19,21,2..., dimensions={0}, use_global_device_ids=true | all-gather | bytes 655360 | tf_op jit(solution)/shard_map/all_gather | solution.py:132
  31.9 3.6 %collective-permute-start.1 = (bf16[128,1024]{1,0:T(8,128)(2,1)S(1)}, bf16[128,1024]{1,0:T(8,128)(2,1)S(1)}, u32[]{:S(2)}, u32[]{:S(2)}) collective-permute-start(bf16[128,1024]{1,0:T(8,128)(2,1)S(1)} %get-tuple-element.9), channel_id=1, source_target_pairs={{7,0},{0,1},{1,2},{2,3},{3,4},{4,5},{5,6},{6,7},{15,8},{8,9},{9,10... | collective-permute-start | bytes 786440 | tf_op jit(solution)/shard_map/ppermute | solution.py:135
  35.5 4.9 %collective-permute-start = (bf16[128,1024]{1,0:T(8,128)(2,1)S(1)}, bf16[128,1024]{1,0:T(8,128)(2,1)S(1)}, u32[]{:S(2)}, u32[]{:S(2)}) collective-permute-start(bf16[128,1024]{1,0:T(8,128)(2,1)S(1)} %get-tuple-element.10), channel_id=1, source_target_pairs={{0,7},{1,0},{2,1},{3,2},{4,3},{5,4},{6,5},{7,6},{8,15},{9,8},{10,9... | collective-permute-start | bytes 786440 | tf_op jit(solution)/shard_map/ppermute | solution.py:134
  40.4 0.1 pad_add_fusion.place_ref
  40.5 2.3 %collective-permute-done.1.high_ref = bf16[128,1024]{1,0:T(8,128)(2,1)S(1)} collective-permute-done((bf16[128,1024]{1,0:T(8,128)(2,1)S(1)}, bf16[128,1024]{1,0:T(8,128)(2,1)S(1)}, u32[]{:S(2)}, u32[]{:S(2)}) %collective-permute-start.1) | collective-permute-done | bytes 262176 | tf_op jit(solution)/shard_map/ppermute | solution.py:135
  42.8 2.1 %collective-permute-done.low_ref = bf16[128,1024]{1,0:T(8,128)(2,1)S(1)} collective-permute-done((bf16[128,1024]{1,0:T(8,128)(2,1)S(1)}, bf16[128,1024]{1,0:T(8,128)(2,1)S(1)}, u32[]{:S(2)}, u32[]{:S(2)}) %collective-permute-start) | collective-permute-done | bytes 262176 | tf_op jit(solution)/shard_map/ppermute | solution.py:134
  45.0 0.0 copy-done
  45.0 1.6 %shard_map.38 = (f32[32,1024]{1,0:T(8,128)S(1)}, f32[32,1024]{1,0:T(8,128)S(1)}) custom-call(s32[2]{0:T(128)S(1)} %pad_add_fusion.place_ref, bf16[256,1024]{1,0:T(8,128)(2,1)S(1)} %bitcast.9, bf16[128,1024]{1,0:T(8,128)(2,1)S(1)} %collective-permute-done.low_ref, bf16[128,1024]{1,0:T(8,128)(2,1)S(1)} %collective-permute-done.1.high_ref, ...), custom_call_target="tpu_custom_call" | custom-call | tf_op jit(solution)/shard_map/pallas_call | solution.py:100
  46.6 1.9 %collective-permute-start.2 = (f32[32,1024]{1,0:T(8,128)S(1)}, f32[32,1024]{1,0:T(8,128)S(1)}, u32[]{:S(2)}, u32[]{:S(2)}) collective-permute-start(f32[32,1024]{1,0:T(8,128)S(1)} %get-tuple-element.7), channel_id=1, source_target_pairs={{16,32},{48,64},{80,96},{112,128},{144,160},{176,192},{208,224},{2... | collective-permute-start | bytes 393224 | tf_op jit(solution)/shard_map/ppermute | solution.py:143
  48.5 3.5 %collective-permute-start.3 = (f32[32,1024]{1,0:T(8,128)S(1)}, f32[32,1024]{1,0:T(8,128)S(1)}, u32[]{:S(2)}, u32[]{:S(2)}) collective-permute-start(f32[32,1024]{1,0:T(8,128)S(1)} %get-tuple-element.8), channel_id=1, source_target_pairs={{0,16},{16,0},{32,48},{48,32},{64,80},{80,64},{96,112},{112,96},{1... | collective-permute-start | bytes 393224 | tf_op jit(solution)/shard_map/ppermute | solution.py:144
  52.0 1.3 %shard_map.37.first_ref = f32[32,1024]{1,0:T(8,128)S(1)} custom-call(s32[2]{0:T(128)S(1)} %pad_add_fusion.place_ref, bf16[256,1024]{1,0:T(8,128)(2,1)S(1)} %bitcast.10, bf16[128,1024]{1,0:T(8,128)(2,1)S(1)} %collective-permute-done.low_ref, bf16[128,1024]{1,0:T(8,128)(2,1)S(1)} %collective-permute-done.1.high_ref, bf16[27,32,512]{2,1,0:T(8,128)(2,1)S(1)} %copy-done), custom_call_target="tpu_custom_call" | custom-call | tf_op jit(solution)/shard_map/pallas_call | solution.py:100
  53.3 0.0 copy-start.1
  53.3 1.7 %collective-permute-done.2.second_ref = f32[32,1024]{1,0:T(8,128)S(1)} collective-permute-done((f32[32,1024]{1,0:T(8,128)S(1)}, f32[32,1024]{1,0:T(8,128)S(1)}, u32[]{:S(2)}, u32[]{:S(2)}) %collective-permute-start.2) | collective-permute-done | bytes 131104 | tf_op jit(solution)/shard_map/ppermute | solution.py:143
  55.0 0.0 collective-permute-done.3
  55.0 0.0 copy-done.1
  55.0 0.7 %fusion = bf16[32,1,1024]{2,0,1:T(8,128)(2,1)} fusion(f32[32,1024]{1,0:T(8,128)S(1)} %shard_map.39, f32[32,1024]{1,0:T(8,128)S(1)} %collective-permute-done.3, f32[32]{0:T(128)S(1)} %copy-done.1), kind=kLoop, calls=%fused_computation.3 | loop fusion | flops 98304 | bytes 327808 | tf_op jit(solution)/shard_map/convert_element_type | solution.py:147
  (2 shorter events, 0.1 us)
Async XLA Ops:
  9.4 35.6 %copy-start = (bf16[27,32,512]{2,1,0:T(8,128)(2,1)S(1)}, bf16[27,32,512]{2,1,0:T(8,128)(2,1)}, u32[]{:S(2)}) copy-start(bf16[27,32,512]{2,1,0:T(8,128)(2,1)} %weight_ref.3) | copy-start | bytes 2654212
  31.9 10.9 %collective-permute-start.1 = (bf16[128,1024]{1,0:T(8,128)(2,1)S(1)}, bf16[128,1024]{1,0:T(8,128)(2,1)S(1)}, u32[]{:S(2)}, u32[]{:S(2)}) collective-permute-start(bf16[128,1024]{1,0:T(8,128)(2,1)S(1)} %get-tuple-element.9), channel_id=1, source_target_pairs={{7,0},{0,1},{1,2},{2,3},{3,4},{4,5},{5,6},{6,7},{15,8},{8,9},{9,10... | collective-permute-start | bytes 786440 | tf_op jit(solution)/shard_map/ppermute | solution.py:135
  35.5 9.5 %collective-permute-start = (bf16[128,1024]{1,0:T(8,128)(2,1)S(1)}, bf16[128,1024]{1,0:T(8,128)(2,1)S(1)}, u32[]{:S(2)}, u32[]{:S(2)}) collective-permute-start(bf16[128,1024]{1,0:T(8,128)(2,1)S(1)} %get-tuple-element.10), channel_id=1, source_target_pairs={{0,7},{1,0},{2,1},{3,2},{4,3},{5,4},{6,5},{7,6},{8,15},{9,8},{10,9... | collective-permute-start | bytes 786440 | tf_op jit(solution)/shard_map/ppermute | solution.py:134
  46.6 8.4 %collective-permute-start.2 = (f32[32,1024]{1,0:T(8,128)S(1)}, f32[32,1024]{1,0:T(8,128)S(1)}, u32[]{:S(2)}, u32[]{:S(2)}) collective-permute-start(f32[32,1024]{1,0:T(8,128)S(1)} %get-tuple-element.7), channel_id=1, source_target_pairs={{16,32},{48,64},{80,96},{112,128},{144,160},{176,192},{208,224},{2... | collective-permute-start | bytes 393224 | tf_op jit(solution)/shard_map/ppermute | solution.py:143
  48.5 6.5 %collective-permute-start.3 = (f32[32,1024]{1,0:T(8,128)S(1)}, f32[32,1024]{1,0:T(8,128)S(1)}, u32[]{:S(2)}, u32[]{:S(2)}) collective-permute-start(f32[32,1024]{1,0:T(8,128)S(1)} %get-tuple-element.8), channel_id=1, source_target_pairs={{0,16},{16,0},{32,48},{48,32},{64,80},{80,64},{96,112},{112,96},{1... | collective-permute-start | bytes 393224 | tf_op jit(solution)/shard_map/ppermute | solution.py:144
  53.3 1.7 %copy-start.1 = (f32[32]{0:T(128)S(1)}, f32[32]{0:T(128)}, u32[]{:S(2)}) copy-start(f32[32]{0:T(128)} %param.5) | copy-start | bytes 388

commit v6 on v3

v6 whole, which is shorter than its diff:
```python
import functools

import jax
import jax.numpy as jnp
from jax import lax
from jax.experimental import pallas as pl
from jax.experimental.pallas import tpu as pltpu
from jax.sharding import PartitionSpec as P

SIDE = 32


def shifted_rows(value, rows):
    cells = value.shape[1]
    place = lax.broadcasted_iota(jnp.int32, value.shape, 1)
    moved = pltpu.roll(value, (rows * SIDE) % cells, 1)
    inside = place >= rows * SIDE if rows > 0 else place < cells + rows * SIDE
    return jnp.where(inside, moved, 0.0)


def shifted_cols(value, cols):
    cells = value.shape[1]
    column = lax.broadcasted_iota(jnp.int32, value.shape, 1) % SIDE
    moved = pltpu.roll(value, cols % cells, 1)
    inside = column >= 1 if cols > 0 else column <= SIDE - 2
    return jnp.where(inside, moved, 0.0)


VMEM = pl.BlockSpec(memory_space=pltpu.VMEM)
PARAMS = pltpu.CompilerParams(vmem_limit_bytes=40 * 1024 * 1024)


def position():
    filt_at = lax.axis_index("filt")
    ring = lax.axis_size("filt") // 2
    return lax.axis_index("slab") % 2, filt_at % 2, filt_at % ring < ring // 2


def picked(rows, parity, block):
    channels = rows.shape[1]
    shape = (channels, channels // 2)
    source = lax.broadcasted_iota(jnp.int32, shape, 0)
    target = lax.broadcasted_iota(jnp.int32, shape, 1)
    side = target // block % 2
    member = target // (2 * block)
    base = side * (channels // 2) + 2 * member * block + target % block
    matrix = jnp.where(source == base + parity * block, 1.0, 0.0).astype(jnp.bfloat16)
    chosen = jnp.dot(rows, matrix, preferred_element_type=jnp.float32)
    return chosen.astype(jnp.bfloat16)


def pick_into(block, parity, weight_ref, own_ref, other_ref, buffer, sem):
    copy = pltpu.make_async_copy(weight_ref, buffer, sem)
    copy.start()
    copy.wait()
    taps, out_rows, channels = buffer.shape
    rows = buffer[...].reshape(taps * out_rows, channels)
    other_ref[...] = picked(rows, 1 - parity, block)
    own_ref[...] = picked(rows, parity, block)


def early_kernel(block, weight_ref, own_ref, send_ref, buffer, sem):
    _, parity, is_early = position()

    @pl.when(is_early)
    def _():
        pick_into(block, parity, weight_ref, own_ref, send_ref, buffer, sem)


def late_kernel(block, weight_ref, early_ref, received_ref, own_ref, other_ref, buffer, sem):
    _, parity, is_early = position()

    @pl.when(is_early)
    def _():
        own_ref[...] = early_ref[...]
        other_ref[...] = received_ref[...]

    @pl.when(jnp.logical_not(is_early))
    def _():
        pick_into(block, parity, weight_ref, own_ref, other_ref, buffer, sem)


def picks(body, block, weights, *early):
    taps, out_rows, channels = weights.shape
    out = jax.ShapeDtypeStruct((taps * out_rows, channels // 2), weights.dtype)
    slow = pl.CostEstimate(flops=10**10, bytes_accessed=0, transcendentals=0)
    return pl.pallas_call(
        functools.partial(body, block),
        out_shape=(out, out),
        in_specs=[pl.BlockSpec(memory_space=pltpu.HBM)] + [VMEM] * len(early),
        out_specs=(VMEM, VMEM),
        scratch_shapes=[pltpu.VMEM(weights.shape, weights.dtype), pltpu.SemaphoreType.DMA],
        compiler_params=PARAMS,
        cost_estimate=slow if early else None,
    )(pltpu.with_memory_space_constraint(weights, pltpu.HBM), *early)


def add_kernel(centre_ref, pair_ref, next_ref, own_ref, other_ref):
    odd, _, _ = position()
    out_rows = own_ref.shape[0]
    total = centre_ref[...] + pair_ref[1 - odd] + next_ref[...]
    other_ref[...] = total[out_rows:]
    own_ref[...] = total[:out_rows]


def added(centre, from_pair, from_next):
    half = jax.ShapeDtypeStruct((centre.shape[0] // 2, centre.shape[1]), centre.dtype)
    return pl.pallas_call(
        add_kernel,
        out_shape=(half, half),
        in_specs=[VMEM] * 3,
        out_specs=(VMEM,) * 2,
        compiler_params=PARAMS,
    )(centre, from_pair, from_next)


def in_plane(product):
    rows = product.shape[0] // 9
    taps = [product[tap * rows : (tap + 1) * rows] for tap in range(9)]
    by_col = [
        taps[3 + col] + shifted_rows(taps[col], 1) + shifted_rows(taps[6 + col], -1)
        for col in range(3)
    ]
    return by_col[1] + shifted_cols(by_col[0], 1) + shifted_cols(by_col[2], -1)


def plane_taps(plane, weight_ref, plane_off):
    rows = weight_ref.shape[0] // 3
    group = weight_ref[pl.ds(plane_off * rows, rows), :]
    return in_plane(jnp.dot(group, plane, preferred_element_type=jnp.float32))


def first_kernel(plane_ref, weight_ref, next_ref, pair_ref):
    plane = plane_ref[...]
    odd, _, _ = position()
    next_ref[...] = plane_taps(plane, weight_ref, 2 - 2 * odd)
    pair_ref[...] = plane_taps(plane, weight_ref, 2 * odd)


def second_kernel(plane_ref, weight_ref, first_next_ref, first_pair_ref, next_ref, pair_ref):
    plane = plane_ref[...]
    odd, _, _ = position()
    out_rows = first_next_ref.shape[0]
    next_ref[:out_rows] = first_next_ref[...]
    pair_ref[:out_rows] = first_pair_ref[...]
    next_ref[out_rows:] = plane_taps(plane, weight_ref, 2 - 2 * odd)
    pair_ref[out_rows:] = plane_taps(plane, weight_ref, 2 * odd)


def centre_kernel(plane_ref, second_ref, own_ref, other_ref, centre_ref):
    out_rows = centre_ref.shape[0] // 2
    centre_ref[:out_rows] = plane_taps(plane_ref[...], own_ref, 1)
    centre_ref[out_rows:] = plane_taps(second_ref[...], other_ref, 1)


def sums(body, out_rows, outs, *args):
    out = jax.ShapeDtypeStruct((out_rows, args[0].shape[1]), jnp.float32)
    return pl.pallas_call(
        body,
        out_shape=(out,) * outs,
        in_specs=[VMEM] * len(args),
        out_specs=(VMEM,) * outs,
        compiler_params=PARAMS,
    )(*args)


def on_device(volume, kernel, channel_bias):
    own_in, planes, cells = volume.shape
    own_out = kernel.shape[1]
    filt = lax.axis_size("filt")
    slabs = lax.axis_size("slab")
    ring = filt // 2
    rings = [[i, i + ring] for i in range(ring)]
    early = [i % ring < ring // 2 for i in range(filt)]
    swap_early = [(i, i ^ 1) for i in range(filt) if early[i]]
    swap_late = [(i, i ^ 1) for i in range(filt) if not early[i]]
    keep_early = [(i, i) for i in range(filt) if early[i]]
    keep_late = [(i, i) for i in range(filt) if not early[i]]
    alike = [
        list(range(half * ring + parity, (half + 1) * ring, 2))
        for half in range(2)
        for parity in range(2)
    ]
    pairs = [[i, i + 1] for i in range(0, slabs, 2)]
    nexts = [(i, i + 1) for i in range(1, slabs - 1, 2)]
    nexts += [(target, source) for source, target in nexts]
    early_own, for_partner = picks(early_kernel, own_in, kernel)
    received = lax.ppermute(for_partner, "filt", swap_early)
    block = volume.reshape(own_in, cells)
    both = lax.all_gather(block, "filt", axis=0, tiled=True, axis_index_groups=rings)
    plane = lax.all_gather(both, "filt", axis=0, tiled=True, axis_index_groups=alike)
    second = lax.ppermute(plane, "filt", keep_early + swap_late)
    own, other = picks(late_kernel, own_in, kernel, early_own, received)

    first = sums(first_kernel, own_out, 2, plane, own)
    to_next, to_pair = sums(second_kernel, 2 * own_out, 2, second, other, *first)
    from_next = lax.ppermute(to_next, "slab", nexts)
    from_pair = lax.all_gather(to_pair, "slab", axis=0, axis_index_groups=pairs)
    (centre,) = sums(centre_kernel, 2 * own_out, 1, plane, second, own, other)
    own_sum, other_sum = added(centre, from_pair, from_next)
    from_other = lax.ppermute(other_sum, "filt", swap_early + keep_late)
    summed = own_sum + from_other + channel_bias[:, None]
    return summed.reshape(own_out, planes, cells).astype(jnp.bfloat16)


def solution(mesh):
    return jax.shard_map(
        on_device,
        mesh=mesh,
        in_specs=(P("filt", "slab", None), P(None, "filt", None), P("filt")),
        out_specs=P("filt", "slab", None),
        check_vma=False,
    )
```

time: 57.4 us -> 54.1 us (0.943)
  the two profiles are of different devices: /device:TPU:56 before, /device:TPU:376 now
where the time goes in v6:
time: 54.1 us; the launch traced here: 53.9 us
  blocking collectives  30.1 us (56%)
  waiting for transfers between devices  13.3 us (25%)
  starting transfers between devices  5.19 us (10%)
  Pallas kernels  4.35 us (8%)
  other arithmetic  0.71 us (1%)
    all_gather x1, blocking collectives, on_device(): lax.all_gather(both, 'filt', axis=0, tiled=True, axis_index_groups=alike)  16.9 us
    all_gather x1, blocking collectives, on_device(): lax.all_gather(block, 'filt', axis=0, tiled=True, axis_index_groups=rings)  9.81 us
    ppermute x1, waiting for transfers between devices, on_device(): second = lax.ppermute(plane, 'filt', keep_early + swap_late)  9.67 us
    ppermute x1, waiting for transfers between devices, on_device(): from_next = lax.ppermute(to_next, 'slab', nexts)  3.66 us
    all_gather x1, blocking collectives, on_device(): from_pair = lax.all_gather(to_pair, 'slab', axis=0, axis_index_groups=pairs)  3.4 us
    pallas_call x3, Pallas kernels, sums(): pl.pallas_call(body, out_shape=(out,) * outs, in_specs=[VMEM] * len(args)...  2.45 us
    ppermute x1, starting transfers between devices, on_device(): from_next = lax.ppermute(to_next, 'slab', nexts)  1.92 us
    ppermute x1, starting transfers between devices, on_device(): second = lax.ppermute(plane, 'filt', keep_early + swap_late)  1.91 us
  transfers between devices with their start and end apart: 4, of which 2 were waited for; matrix products, arithmetic and copies ran while one was open for 0% of the time, Pallas kernels for 6%

profile of v6, /device:TPU:376, one launch (start us, length us, event | category | flops | bytes accessed | tf_op | source)
XLA Modules:
  0.0 53.9 jit_solution(4409987795605756538)
XLA Ops:
  0.0 0.0 copy-start
  0.0 0.7 %collective-permute-start.1 = (bf16[864,256]{1,0:T(8,128)(2,1)S(1)}, bf16[864,256]{1,0:T(8,128)(2,1)S(1)}, u32[]{:S(2)}, u32[]{:S(2)}) collective-permute-start(bf16[864,256]{1,0:T(8,128)(2,1)S(1)} %get-tuple-element.16), channel_id=1, source_target_pairs={{0,1},{1,0},{2,3},{3,2},{8,9},{9,8},{10,11},{11,10},{16,17},{17,16... | collective-permute-start | bytes 1327112 | tf_op jit(solution)/shard_map/ppermute | solution.py:188
  0.7 0.1 copy-done
  0.8 9.8 %all-gather = bf16[64,1,1024]{2,0,1:T(8,128)(2,1)S(1)} all-gather(bf16[32,1,1024]{2,0,1:T(8,128)(2,1)S(1)} %copy-done), channel_id=2, replica_groups={{0,8},{1,9},{2,10},{3,11},{4,12},{5,13},{6,14},{7,15},{16,24},{17,25},{..., dimensions={0}, use_global_device_ids=true | all-gather | bytes 196608 | tf_op jit(solution)/shard_map/all_gather | solution.py:190
  10.6 16.9 %all-gather.1 = bf16[256,1,1024]{2,0,1:T(8,128)(2,1)S(1)} all-gather(bf16[64,1,1024]{2,0,1:T(8,128)(2,1)S(1)} %all-gather), channel_id=3, replica_groups={{0,2,4,6},{1,3,5,7},{8,10,12,14},{9,11,13,15},{16,18,20,22},{17,19,21,2..., dimensions={0}, use_global_device_ids=true | all-gather | bytes 655360 | tf_op jit(solution)/shard_map/all_gather | solution.py:191
  27.5 1.9 %collective-permute-start = (bf16[256,1024]{1,0:T(8,128)(2,1)S(1)}, bf16[256,1024]{1,0:T(8,128)(2,1)S(1)}, u32[]{:S(2)}, u32[]{:S(2)}) collective-permute-start(bf16[256,1024]{1,0:T(8,128)(2,1)S(1)} %bitcast.4), channel_id=1, source_target_pairs={{0,0},{1,1},{2,2},{3,3},{8,8},{9,9},{10,10},{11,11},{4,5},{5,4},{6... | collective-permute-start | bytes 1572872 | tf_op jit(solution)/shard_map/ppermute | solution.py:192
  29.4 0.0 collective-permute-done.1.received_ref
  29.4 1.9 %shard_map.38 = (bf16[864,256]{1,0:T(8,128)(2,1)S(1)}, bf16[864,256]{1,0:T(8,128)(2,1)S(1)}) custom-call(bf16[27,32,512]{2,1,0:T(8,128)(2,1)} %weight_ref.3, bf16[864,256]{1,0:T(8,128)(2,1)S(1)} %get-tuple-element.15.early_ref, bf16[864,256]{1,0:T(8,128)(2,1)S(1)} %collective-permute-done.1.received_ref), custom_call_target="tpu_custom_call" | custom-call | flops 10000000000 | tf_op jit(solution)/shard_map/pallas_call | solution.py:87
  31.3 0.8 %shard_map.40 = (f32[32,1024]{1,0:T(8,128)S(1)}, f32[32,1024]{1,0:T(8,128)S(1)}) custom-call(bf16[256,1024]{1,0:T(8,128)(2,1)S(1)} %bitcast.5, bf16[864,256]{1,0:T(8,128)(2,1)S(1)} %get-tuple-element.17.own_ref.weight_ref), custom_call_target="tpu_custom_call" | custom-call | tf_op jit(solution)/shard_map/pallas_call | solution.py:158
  32.1 9.7 %collective-permute-done.second_ref.plane_ref = bf16[256,1024]{1,0:T(8,128)(2,1)S(1)} collective-permute-done((bf16[256,1024]{1,0:T(8,128)(2,1)S(1)}, bf16[256,1024]{1,0:T(8,128)(2,1)S(1)}, u32[]{:S(2)}, u32[]{:S(2)}) %collective-permute-start) | collective-permute-done | bytes 524320 | tf_op jit(solution)/shard_map/ppermute | solution.py:192
  41.8 0.8 %shard_map.41 = (f32[64,1024]{1,0:T(8,128)S(1)}, f32[64,1024]{1,0:T(8,128)S(1)}) custom-call(bf16[256,1024]{1,0:T(8,128)(2,1)S(1)} %collective-permute-done.second_ref.plane_ref, bf16[864,256]{1,0:T(8,128)(2,1)S(1)} %get-tuple-element.18.other_ref.weight_ref, f32[32,1024]{1,0:T(8,128)S(1)} %get-tuple-element.19.first_next_ref, ...), custom_call_target="tpu_custom_call" | custom-call | tf_op jit(solution)/shard_map/pallas_call | solution.py:158
  42.6 1.9 %collective-permute-start.2 = (f32[64,1024]{1,0:T(8,128)S(1)}, f32[64,1024]{1,0:T(8,128)S(1)}, u32[]{:S(2)}, u32[]{:S(2)}) collective-permute-start(f32[64,1024]{1,0:T(8,128)S(1)} %get-tuple-element.22), channel_id=1, source_target_pairs={{16,32},{48,64},{80,96},{112,128},{144,160},{176,192},{208,224},{2... | collective-permute-start | bytes 786440 | tf_op jit(solution)/shard_map/ppermute | solution.py:197
  44.6 0.8 %shard_map.39.centre_ref = f32[64,1024]{1,0:T(8,128)S(1)} custom-call(bf16[256,1024]{1,0:T(8,128)(2,1)S(1)} %bitcast.6, bf16[256,1024]{1,0:T(8,128)(2,1)S(1)} %collective-permute-done.second_ref.plane_ref, bf16[864,256]{1,0:T(8,128)(2,1)S(1)} %get-tuple-element.17.own_ref.weight_ref, bf16[864,256]{1,0:T(8,128)(2,1)S(1)} %get-tuple-element.18.other_ref.weight_ref), custom_call_target="tpu_custom_call" | custom-call | tf_op jit(solution)/shard_map/pallas_call | solution.py:158
  45.4 3.4 %all-gather.2 = f32[128,1024]{1,0:T(8,128)S(1)} all-gather(f32[64,1024]{1,0:T(8,128)S(1)} %get-tuple-element.21), channel_id=4, replica_groups={{0,16},{32,48},{64,80},{96,112},{128,144},{160,176},{192,208},{224,240}..., dimensions={0}, use_global_device_ids=true | all-gather | bytes 786432 | tf_op jit(solution)/shard_map/all_gather | solution.py:198
  48.8 3.7 %collective-permute-done.2.next_ref = f32[64,1024]{1,0:T(8,128)S(1)} collective-permute-done((f32[64,1024]{1,0:T(8,128)S(1)}, f32[64,1024]{1,0:T(8,128)S(1)}, u32[]{:S(2)}, u32[]{:S(2)}) %collective-permute-start.2) | collective-permute-done | bytes 262176 | tf_op jit(solution)/shard_map/ppermute | solution.py:197
  52.5 0.0 copy-start.1
  52.5 0.7 %collective-permute-start.3 = (f32[32,1024]{1,0:T(8,128)S(1)}, f32[32,1024]{1,0:T(8,128)S(1)}, u32[]{:S(2)}, u32[]{:S(2)}) collective-permute-start(f32[32,1024]{1,0:T(8,128)S(1)} %get-tuple-element.24), channel_id=1, source_target_pairs={{0,1},{1,0},{2,3},{3,2},{8,9},{9,8},{10,11},{11,10},{4,4},{5,5},{6... | collective-permute-start | bytes 393224 | tf_op jit(solution)/shard_map/ppermute | solution.py:201
  53.2 0.0 collective-permute-done.3
  53.2 0.0 copy-done.1
  53.2 0.7 %fusion = bf16[32,1,1024]{2,0,1:T(8,128)(2,1)} fusion(f32[32,1024]{1,0:T(8,128)S(1)} %get-tuple-element.23, f32[32,1024]{1,0:T(8,128)S(1)} %collective-permute-done.3, f32[32]{0:T(128)S(1)} %copy-done.1), kind=kLoop, calls=%fused_computation.1 | loop fusion | flops 98304 | bytes 327808 | tf_op jit(solution)/shard_map/convert_element_type | solution.py:203
  (2 shorter events, 0.0 us)
Async XLA Ops:
  0.0 0.8 %copy-start = (bf16[32,1,1024]{2,0,1:T(8,128)(2,1)S(1)}, bf16[32,1,1024]{2,0,1:T(8,128)(2,1)}, u32[]{:S(2)}) copy-start(bf16[32,1,1024]{2,0,1:T(8,128)(2,1)} %param.3) | copy-start | bytes 196612
  0.0 29.4 %collective-permute-start.1 = (bf16[864,256]{1,0:T(8,128)(2,1)S(1)}, bf16[864,256]{1,0:T(8,128)(2,1)S(1)}, u32[]{:S(2)}, u32[]{:S(2)}) collective-permute-start(bf16[864,256]{1,0:T(8,128)(2,1)S(1)} %get-tuple-element.16), channel_id=1, source_target_pairs={{0,1},{1,0},{2,3},{3,2},{8,9},{9,8},{10,11},{11,10},{16,17},{17,16... | collective-permute-start | bytes 1327112 | tf_op jit(solution)/shard_map/ppermute | solution.py:188
  27.5 14.3 %collective-permute-start = (bf16[256,1024]{1,0:T(8,128)(2,1)S(1)}, bf16[256,1024]{1,0:T(8,128)(2,1)S(1)}, u32[]{:S(2)}, u32[]{:S(2)}) collective-permute-start(bf16[256,1024]{1,0:T(8,128)(2,1)S(1)} %bitcast.4), channel_id=1, source_target_pairs={{0,0},{1,1},{2,2},{3,3},{8,8},{9,9},{10,10},{11,11},{4,5},{5,4},{6... | collective-permute-start | bytes 1572872 | tf_op jit(solution)/shard_map/ppermute | solution.py:192
  42.6 9.8 %collective-permute-start.2 = (f32[64,1024]{1,0:T(8,128)S(1)}, f32[64,1024]{1,0:T(8,128)S(1)}, u32[]{:S(2)}, u32[]{:S(2)}) collective-permute-start(f32[64,1024]{1,0:T(8,128)S(1)} %get-tuple-element.22), channel_id=1, source_target_pairs={{16,32},{48,64},{80,96},{112,128},{144,160},{176,192},{208,224},{2... | collective-permute-start | bytes 786440 | tf_op jit(solution)/shard_map/ppermute | solution.py:197
  52.5 0.7 %copy-start.1 = (f32[32]{0:T(128)S(1)}, f32[32]{0:T(128)}, u32[]{:S(2)}) copy-start(f32[32]{0:T(128)} %param.5) | copy-start | bytes 388
  52.5 0.7 %collective-permute-start.3 = (f32[32,1024]{1,0:T(8,128)S(1)}, f32[32,1024]{1,0:T(8,128)S(1)}, u32[]{:S(2)}, u32[]{:S(2)}) collective-permute-start(f32[32,1024]{1,0:T(8,128)S(1)} %get-tuple-element.24), channel_id=1, source_target_pairs={{0,1},{1,0},{2,3},{3,2},{8,9},{9,8},{10,11},{11,10},{4,4},{5,5},{6... | collective-permute-start | bytes 393224 | tf_op jit(solution)/shard_map/ppermute | solution.py:201

commit v7 on v6

--- a/solution.py
+++ b/solution.py
@@ -95,23 +95,23 @@
     )(pltpu.with_memory_space_constraint(weights, pltpu.HBM), *early)
 
 
-def add_kernel(centre_ref, pair_ref, next_ref, own_ref, other_ref):
+def add_kernel(centre_ref, pair_ref, late_next_ref, early_next_ref, own_ref, other_ref):
     odd, _, _ = position()
     out_rows = own_ref.shape[0]
-    total = centre_ref[...] + pair_ref[1 - odd] + next_ref[...]
+    total = centre_ref[...] + pair_ref[1 - odd] + early_next_ref[...]
     other_ref[...] = total[out_rows:]
-    own_ref[...] = total[:out_rows]
-
-
-def added(centre, from_pair, from_next):
+    own_ref[...] = total[:out_rows] + late_next_ref[...]
+
+
+def added(centre, *parts):
     half = jax.ShapeDtypeStruct((centre.shape[0] // 2, centre.shape[1]), centre.dtype)
     return pl.pallas_call(
         add_kernel,
         out_shape=(half, half),
-        in_specs=[VMEM] * 3,
+        in_specs=[VMEM] * (1 + len(parts)),
         out_specs=(VMEM,) * 2,
         compiler_params=PARAMS,
-    )(centre, from_pair, from_next)
+    )(centre, *parts)
 
 
 def in_plane(product):
@@ -137,29 +137,40 @@
     pair_ref[...] = plane_taps(plane, weight_ref, 2 * odd)
 
 
-def second_kernel(plane_ref, weight_ref, first_next_ref, first_pair_ref, next_ref, pair_ref):
+def shared(second):
+    _, _, is_early = position()
+    return jnp.where(is_early, jnp.zeros_like(second), second)
+
+
+def second_kernel(
+    plane_ref, weight_ref, first_next_ref, first_pair_ref, late_next_ref, early_next_ref, pair_ref
+):
     plane = plane_ref[...]
     odd, _, _ = position()
     out_rows = first_next_ref.shape[0]
-    next_ref[:out_rows] = first_next_ref[...]
-    pair_ref[:out_rows] = first_pair_ref[...]
-    next_ref[out_rows:] = plane_taps(plane, weight_ref, 2 - 2 * odd)
-    pair_ref[out_rows:] = plane_taps(plane, weight_ref, 2 * odd)
+    away = plane_taps(plane, weight_ref, 2 - 2 * odd)
+    late_next_ref[...] = first_next_ref[...] + away
+    early_next_ref[:out_rows] = first_next_ref[...]
+    early_next_ref[out_rows:] = away
+    across = plane_taps(plane, weight_ref, 2 * odd)
+    pair_ref[:out_rows] = first_pair_ref[...] + shared(across)
+    pair_ref[out_rows:] = across
 
 
 def centre_kernel(plane_ref, second_ref, own_ref, other_ref, centre_ref):
     out_rows = centre_ref.shape[0] // 2
-    centre_ref[:out_rows] = plane_taps(plane_ref[...], own_ref, 1)
-    centre_ref[out_rows:] = plane_taps(second_ref[...], other_ref, 1)
-
-
-def sums(body, out_rows, outs, *args):
-    out = jax.ShapeDtypeStruct((out_rows, args[0].shape[1]), jnp.float32)
+    second = plane_taps(second_ref[...], other_ref, 1)
+    centre_ref[:out_rows] = plane_taps(plane_ref[...], own_ref, 1) + shared(second)
+    centre_ref[out_rows:] = second
+
+
+def sums(body, out_rows, *args):
+    cells = args[0].shape[1]
     return pl.pallas_call(
         body,
-        out_shape=(out,) * outs,
+        out_shape=tuple(jax.ShapeDtypeStruct((rows, cells), jnp.float32) for rows in out_rows),
         in_specs=[VMEM] * len(args),
-        out_specs=(VMEM,) * outs,
+        out_specs=(VMEM,) * len(out_rows),
         compiler_params=PARAMS,
     )(*args)
 
@@ -175,7 +186,6 @@
     swap_early = [(i, i ^ 1) for i in range(filt) if early[i]]
     swap_late = [(i, i ^ 1) for i in range(filt) if not early[i]]
     keep_early = [(i, i) for i in range(filt) if early[i]]
-    keep_late = [(i, i) for i in range(filt) if not early[i]]
     alike = [
         list(range(half * ring + parity, (half + 1) * ring, 2))
         for half in range(2)
@@ -184,6 +194,15 @@
     pairs = [[i, i + 1] for i in range(0, slabs, 2)]
     nexts = [(i, i + 1) for i in range(1, slabs - 1, 2)]
     nexts += [(target, source) for source, target in nexts]
+
+    def crossing(members):
+        return [
+            (source * filt + i, target * filt + i)
+            for source, target in nexts
+            for i in range(filt)
+            if members[i]
+        ]
+
     early_own, for_partner = picks(early_kernel, own_in, kernel)
     received = lax.ppermute(for_partner, "filt", swap_early)
     block = volume.reshape(own_in, cells)
@@ -192,13 +211,17 @@
     second = lax.ppermute(plane, "filt", keep_early + swap_late)
     own, other = picks(late_kernel, own_in, kernel, early_own, received)
 
-    first = sums(first_kernel, own_out, 2, plane, own)
-    to_next, to_pair = sums(second_kernel, 2 * own_out, 2, second, other, *first)
-    from_next = lax.ppermute(to_next, "slab", nexts)
+    first = sums(first_kernel, (own_out, own_out), plane, own)
+    late_to_next, early_to_next, to_pair = sums(
+        second_kernel, (own_out, 2 * own_out, 2 * own_out), second, other, *first
+    )
+    both_axes = ("slab", "filt")
+    early_from_next = lax.ppermute(early_to_next, both_axes, crossing(early))
+    late_from_next = lax.ppermute(late_to_next, both_axes, crossing([not e for e in early]))
     from_pair = lax.all_gather(to_pair, "slab", axis=0, axis_index_groups=pairs)
-    (centre,) = sums(centre_kernel, 2 * own_out, 1, plane, second, own, other)
-    own_sum, other_sum = added(centre, from_pair, from_next)
-    from_other = lax.ppermute(other_sum, "filt", swap_early + keep_late)
+    (centre,) = sums(centre_kernel, (2 * own_out,), plane, second, own, other)
+    own_sum, other_sum = added(centre, from_pair, late_from_next, early_from_next)
+    from_other = lax.ppermute(other_sum, "filt", swap_early)
     summed = own_sum + from_other + channel_bias[:, None]
     return summed.reshape(own_out, planes, cells).astype(jnp.bfloat16)
 

time: 54.1 us -> 53.5 us (0.989)
  the two profiles are of different devices: /device:TPU:376 before, /device:TPU:56 now
where the time goes in v7:
time: 53.5 us; the launch traced here: 52.8 us
  blocking collectives  30.1 us (56%)
  starting transfers between devices  10.9 us (20%)
  waiting for transfers between devices  6.45 us (12%)
  Pallas kernels  4.47 us (8%)
  other arithmetic  0.71 us (1%)
    all_gather x1, blocking collectives, on_device(): lax.all_gather(both, 'filt', axis=0, tiled=True, axis_index_groups=alike)  17.2 us
    all_gather x1, blocking collectives, on_device(): lax.all_gather(block, 'filt', axis=0, tiled=True, axis_index_groups=rings)  9.55 us
    ppermute x1, starting transfers between devices, on_device(): received = lax.ppermute(for_partner, 'filt', swap_early)  4.28 us
    ppermute x1, waiting for transfers between devices, on_device(): from_other = lax.ppermute(other_sum, 'filt', swap_early)  3.49 us
    all_gather x1, blocking collectives, on_device(): from_pair = lax.all_gather(to_pair, 'slab', axis=0, axis_index_groups=pairs)  3.4 us
    ppermute x1, starting transfers between devices, on_device(): from_other = lax.ppermute(other_sum, 'filt', swap_early)  3.37 us
    ppermute x1, waiting for transfers between devices, on_device(): early_from_next = lax.ppermute(early_to_next, both_axes, crossing(early))  2.96 us
    pallas_call x3, Pallas kernels, sums(): pl.pallas_call(body, out_shape=tuple((jax.ShapeDtypeStruct((rows, cells),...  2.47 us
  transfers between devices with their start and end apart: 5, of which 2 were waited for; matrix products, arithmetic and copies ran while one was open for 0% of the time, Pallas kernels for 3%

profile of v7, /device:TPU:56, one launch (start us, length us, event | category | flops | bytes accessed | tf_op | source)
XLA Modules:
  0.0 52.8 jit_solution(6067490149625081781)
XLA Ops:
  0.0 0.0 copy-start
  0.0 1.9 %shard_map.37 = (bf16[864,256]{1,0:T(8,128)(2,1)S(1)}, bf16[864,256]{1,0:T(8,128)(2,1)S(1)}) custom-call(bf16[27,32,512]{2,1,0:T(8,128)(2,1)} %weight_ref.3), custom_call_target="tpu_custom_call" | custom-call | tf_op jit(solution)/shard_map/pallas_call | solution.py:87
  1.9 4.3 %collective-permute-start.1 = (bf16[864,256]{1,0:T(8,128)(2,1)S(1)}, bf16[864,256]{1,0:T(8,128)(2,1)S(1)}, u32[]{:S(2)}, u32[]{:S(2)}) collective-permute-start(bf16[864,256]{1,0:T(8,128)(2,1)S(1)} %get-tuple-element.17), channel_id=1, source_target_pairs={{0,1},{1,0},{2,3},{3,2},{8,9},{9,8},{10,11},{11,10},{16,17},{17,16... | collective-permute-start | bytes 1327112 | tf_op jit(solution)/shard_map/ppermute | solution.py:207
  6.2 0.0 copy-done
  6.2 9.6 %all-gather = bf16[64,1,1024]{2,0,1:T(8,128)(2,1)S(1)} all-gather(bf16[32,1,1024]{2,0,1:T(8,128)(2,1)S(1)} %copy-done), channel_id=2, replica_groups={{0,8},{1,9},{2,10},{3,11},{4,12},{5,13},{6,14},{7,15},{16,24},{17,25},{..., dimensions={0}, use_global_device_ids=true | all-gather | bytes 196608 | tf_op jit(solution)/shard_map/all_gather | solution.py:209
  15.7 17.2 %all-gather.1 = bf16[256,1,1024]{2,0,1:T(8,128)(2,1)S(1)} all-gather(bf16[64,1,1024]{2,0,1:T(8,128)(2,1)S(1)} %all-gather), channel_id=3, replica_groups={{0,2,4,6},{1,3,5,7},{8,10,12,14},{9,11,13,15},{16,18,20,22},{17,19,21,2..., dimensions={0}, use_global_device_ids=true | all-gather | bytes 655360 | tf_op jit(solution)/shard_map/all_gather | solution.py:210
  32.9 0.7 %collective-permute-start = (bf16[256,1024]{1,0:T(8,128)(2,1)S(1)}, bf16[256,1024]{1,0:T(8,128)(2,1)S(1)}, u32[]{:S(2)}, u32[]{:S(2)}) collective-permute-start(bf16[256,1024]{1,0:T(8,128)(2,1)S(1)} %bitcast.4), channel_id=1, source_target_pairs={{0,0},{1,1},{2,2},{3,3},{8,8},{9,9},{10,10},{11,11},{4,5},{5,4},{6... | collective-permute-start | bytes 1572872 | tf_op jit(solution)/shard_map/ppermute | solution.py:211
  33.6 0.0 collective-permute-done.1.received_ref
  33.6 0.1 shard_map.38
  33.7 0.8 %shard_map.40 = (f32[32,1024]{1,0:T(8,128)S(1)}, f32[32,1024]{1,0:T(8,128)S(1)}) custom-call(bf16[256,1024]{1,0:T(8,128)(2,1)S(1)} %bitcast.5, bf16[864,256]{1,0:T(8,128)(2,1)S(1)} %get-tuple-element.18.own_ref.weight_ref), custom_call_target="tpu_custom_call" | custom-call | tf_op jit(solution)/shard_map/pallas_call | solution.py:169
  34.5 0.0 collective-permute-done.second_ref.plane_ref
  34.5 0.8 %shard_map.41 = (f32[32,1024]{1,0:T(8,128)S(1)}, f32[64,1024]{1,0:T(8,128)S(1)}, f32[64,1024]{1,0:T(8,128)S(1)}) custom-call(bf16[256,1024]{1,0:T(8,128)(2,1)S(1)} %collective-permute-done.second_ref.plane_ref, bf16[864,256]{1,0:T(8,128)(2,1)S(1)} %get-tuple-element.19.other_ref.weight_ref, f32[32,1024]{1,0:T(8,128)S(1)} %get-tuple-element.20.first_next_ref, ...), custom_call_target="tpu_custom_call" | custom-call | tf_op jit(solution)/shard_map/pallas_call | solution.py:169
  35.4 1.9 %collective-permute-start.3 = (f32[64,1024]{1,0:T(8,128)S(1)}, f32[64,1024]{1,0:T(8,128)S(1)}, u32[]{:S(2)}, u32[]{:S(2)}) collective-permute-start(f32[64,1024]{1,0:T(8,128)S(1)} %get-tuple-element.24), channel_id=1, source_target_pairs={{16,32},{17,33},{18,34},{19,35},{24,40},{25,41},{26,42},{27,43},{4... | collective-permute-start | bytes 786440 | tf_op jit(solution)/shard_map/ppermute | solution.py:219
  37.3 0.7 %collective-permute-start.2 = (f32[32,1024]{1,0:T(8,128)S(1)}, f32[32,1024]{1,0:T(8,128)S(1)}, u32[]{:S(2)}, u32[]{:S(2)}) collective-permute-start(f32[32,1024]{1,0:T(8,128)S(1)} %get-tuple-element.23), channel_id=1, source_target_pairs={{20,36},{21,37},{22,38},{23,39},{28,44},{29,45},{30,46},{31,47},{5... | collective-permute-start | bytes 393224 | tf_op jit(solution)/shard_map/ppermute | solution.py:220
  38.0 0.8 %shard_map.39.centre_ref = f32[64,1024]{1,0:T(8,128)S(1)} custom-call(bf16[256,1024]{1,0:T(8,128)(2,1)S(1)} %bitcast.6, bf16[256,1024]{1,0:T(8,128)(2,1)S(1)} %collective-permute-done.second_ref.plane_ref, bf16[864,256]{1,0:T(8,128)(2,1)S(1)} %get-tuple-element.18.own_ref.weight_ref, bf16[864,256]{1,0:T(8,128)(2,1)S(1)} %get-tuple-element.19.other_ref.weight_ref), custom_call_target="tpu_custom_call" | custom-call | tf_op jit(solution)/shard_map/pallas_call | solution.py:169
  38.8 3.4 %all-gather.2 = f32[128,1024]{1,0:T(8,128)S(1)} all-gather(f32[64,1024]{1,0:T(8,128)S(1)} %get-tuple-element.22), channel_id=4, replica_groups={{0,16},{32,48},{64,80},{96,112},{128,144},{160,176},{192,208},{224,240}..., dimensions={0}, use_global_device_ids=true | all-gather | bytes 786432 | tf_op jit(solution)/shard_map/all_gather | solution.py:221
  42.2 0.0 collective-permute-done.2.late_next_ref
  42.2 3.0 %collective-permute-done.3.early_next_ref = f32[64,1024]{1,0:T(8,128)S(1)} collective-permute-done((f32[64,1024]{1,0:T(8,128)S(1)}, f32[64,1024]{1,0:T(8,128)S(1)}, u32[]{:S(2)}, u32[]{:S(2)}) %collective-permute-start.3) | collective-permute-done | bytes 262176 | tf_op jit(solution)/shard_map/ppermute | solution.py:219
  45.2 0.0 copy-start.1
  45.2 3.4 %collective-permute-start.4 = (f32[32,1024]{1,0:T(8,128)S(1)}, f32[32,1024]{1,0:T(8,128)S(1)}, u32[]{:S(2)}, u32[]{:S(2)}) collective-permute-start(f32[32,1024]{1,0:T(8,128)S(1)} %get-tuple-element.26), channel_id=1, source_target_pairs={{0,1},{1,0},{2,3},{3,2},{8,9},{9,8},{10,11},{11,10},{16,17},{17,16... | collective-permute-start | bytes 393224 | tf_op jit(solution)/shard_map/ppermute | solution.py:224
  48.6 3.5 %collective-permute-done.4 = f32[32,1024]{1,0:T(8,128)S(1)} collective-permute-done((f32[32,1024]{1,0:T(8,128)S(1)}, f32[32,1024]{1,0:T(8,128)S(1)}, u32[]{:S(2)}, u32[]{:S(2)}) %collective-permute-start.4) | collective-permute-done | bytes 131104 | tf_op jit(solution)/shard_map/ppermute | solution.py:224
  52.1 0.0 copy-done.1
  52.1 0.7 %fusion = bf16[32,1,1024]{2,0,1:T(8,128)(2,1)} fusion(f32[32,1024]{1,0:T(8,128)S(1)} %get-tuple-element.25, f32[32,1024]{1,0:T(8,128)S(1)} %collective-permute-done.4, f32[32]{0:T(128)S(1)} %copy-done.1), kind=kLoop, calls=%fused_computation.1 | loop fusion | flops 98304 | bytes 327808 | tf_op jit(solution)/shard_map/convert_element_type | solution.py:226
  (1 shorter events, 0.0 us)
Async XLA Ops:
  0.0 6.2 %copy-start = (bf16[32,1,1024]{2,0,1:T(8,128)(2,1)S(1)}, bf16[32,1,1024]{2,0,1:T(8,128)(2,1)}, u32[]{:S(2)}) copy-start(bf16[32,1,1024]{2,0,1:T(8,128)(2,1)} %param.3) | copy-start | bytes 196612
  1.9 31.7 %collective-permute-start.1 = (bf16[864,256]{1,0:T(8,128)(2,1)S(1)}, bf16[864,256]{1,0:T(8,128)(2,1)S(1)}, u32[]{:S(2)}, u32[]{:S(2)}) collective-permute-start(bf16[864,256]{1,0:T(8,128)(2,1)S(1)} %get-tuple-element.17), channel_id=1, source_target_pairs={{0,1},{1,0},{2,3},{3,2},{8,9},{9,8},{10,11},{11,10},{16,17},{17,16... | collective-permute-start | bytes 1327112 | tf_op jit(solution)/shard_map/ppermute | solution.py:207
  32.9 1.6 %collective-permute-start = (bf16[256,1024]{1,0:T(8,128)(2,1)S(1)}, bf16[256,1024]{1,0:T(8,128)(2,1)S(1)}, u32[]{:S(2)}, u32[]{:S(2)}) collective-permute-start(bf16[256,1024]{1,0:T(8,128)(2,1)S(1)} %bitcast.4), channel_id=1, source_target_pairs={{0,0},{1,1},{2,2},{3,3},{8,8},{9,9},{10,10},{11,11},{4,5},{5,4},{6... | collective-permute-start | bytes 1572872 | tf_op jit(solution)/shard_map/ppermute | solution.py:211
  35.4 9.8 %collective-permute-start.3 = (f32[64,1024]{1,0:T(8,128)S(1)}, f32[64,1024]{1,0:T(8,128)S(1)}, u32[]{:S(2)}, u32[]{:S(2)}) collective-permute-start(f32[64,1024]{1,0:T(8,128)S(1)} %get-tuple-element.24), channel_id=1, source_target_pairs={{16,32},{17,33},{18,34},{19,35},{24,40},{25,41},{26,42},{27,43},{4... | collective-permute-start | bytes 786440 | tf_op jit(solution)/shard_map/ppermute | solution.py:219
  37.3 4.9 %collective-permute-start.2 = (f32[32,1024]{1,0:T(8,128)S(1)}, f32[32,1024]{1,0:T(8,128)S(1)}, u32[]{:S(2)}, u32[]{:S(2)}) collective-permute-start(f32[32,1024]{1,0:T(8,128)S(1)} %get-tuple-element.23), channel_id=1, source_target_pairs={{20,36},{21,37},{22,38},{23,39},{28,44},{29,45},{30,46},{31,47},{5... | collective-permute-start | bytes 393224 | tf_op jit(solution)/shard_map/ppermute | solution.py:220
  45.2 6.9 %copy-start.1 = (f32[32]{0:T(128)S(1)}, f32[32]{0:T(128)}, u32[]{:S(2)}) copy-start(f32[32]{0:T(128)} %param.5) | copy-start | bytes 388
  45.2 6.9 %collective-permute-start.4 = (f32[32,1024]{1,0:T(8,128)S(1)}, f32[32,1024]{1,0:T(8,128)S(1)}, u32[]{:S(2)}, u32[]{:S(2)}) collective-permute-start(f32[32,1024]{1,0:T(8,128)S(1)} %get-tuple-element.26), channel_id=1, source_target_pairs={{0,1},{1,0},{2,3},{3,2},{8,9},{9,8},{10,11},{11,10},{16,17},{17,16... | collective-permute-start | bytes 393224 | tf_op jit(solution)/shard_map/ppermute | solution.py:224

commit v8 on v7

--- a/solution.py
+++ b/solution.py
@@ -12,7 +12,7 @@
 
 def shifted_rows(value, rows):
     cells = value.shape[1]
-    place = lax.broadcasted_iota(jnp.int32, value.shape, 1)
+    place = lax.broadcasted_iota(jnp.int32, (1, cells), 1)
     moved = pltpu.roll(value, (rows * SIDE) % cells, 1)
     inside = place >= rows * SIDE if rows > 0 else place < cells + rows * SIDE
     return jnp.where(inside, moved, 0.0)
@@ -20,7 +20,7 @@
 
 def shifted_cols(value, cols):
     cells = value.shape[1]
-    column = lax.broadcasted_iota(jnp.int32, value.shape, 1) % SIDE
+    column = lax.broadcasted_iota(jnp.int32, (1, cells), 1) & (SIDE - 1)
     moved = pltpu.roll(value, cols % cells, 1)
     inside = column >= 1 if cols > 0 else column <= SIDE - 2
     return jnp.where(inside, moved, 0.0)
@@ -38,13 +38,12 @@
 
 def picked(rows, parity, block):
     channels = rows.shape[1]
-    shape = (channels, channels // 2)
-    source = lax.broadcasted_iota(jnp.int32, shape, 0)
-    target = lax.broadcasted_iota(jnp.int32, shape, 1)
+    source = lax.broadcasted_iota(jnp.int32, (channels, channels // 2), 0)
+    target = lax.broadcasted_iota(jnp.int32, (1, channels // 2), 1)
     side = target // block % 2
     member = target // (2 * block)
-    base = side * (channels // 2) + 2 * member * block + target % block
-    matrix = jnp.where(source == base + parity * block, 1.0, 0.0).astype(jnp.bfloat16)
+    wanted = side * (channels // 2) + (2 * member + parity) * block + target % block
+    matrix = jnp.where(source == wanted, 1.0, 0.0).astype(jnp.bfloat16)
     chosen = jnp.dot(rows, matrix, preferred_element_type=jnp.float32)
     return chosen.astype(jnp.bfloat16)
 
@@ -95,10 +94,9 @@
     )(pltpu.with_memory_space_constraint(weights, pltpu.HBM), *early)
 
 
-def add_kernel(centre_ref, pair_ref, late_next_ref, early_next_ref, own_ref, other_ref):
-    odd, _, _ = position()
+def add_kernel(centre_ref, late_next_ref, early_next_ref, own_ref, other_ref):
     out_rows = own_ref.shape[0]
-    total = centre_ref[...] + pair_ref[1 - odd] + early_next_ref[...]
+    total = centre_ref[...] + early_next_ref[...]
     other_ref[...] = total[out_rows:]
     own_ref[...] = total[:out_rows] + late_next_ref[...]
 
@@ -142,26 +140,31 @@
     return jnp.where(is_early, jnp.zeros_like(second), second)
 
 
-def second_kernel(
-    plane_ref, weight_ref, first_next_ref, first_pair_ref, late_next_ref, early_next_ref, pair_ref
-):
-    plane = plane_ref[...]
-    odd, _, _ = position()
-    out_rows = first_next_ref.shape[0]
-    away = plane_taps(plane, weight_ref, 2 - 2 * odd)
-    late_next_ref[...] = first_next_ref[...] + away
-    early_next_ref[:out_rows] = first_next_ref[...]
-    early_next_ref[out_rows:] = away
-    across = plane_taps(plane, weight_ref, 2 * odd)
-    pair_ref[:out_rows] = first_pair_ref[...] + shared(across)
-    pair_ref[out_rows:] = across
-
-
-def centre_kernel(plane_ref, second_ref, own_ref, other_ref, centre_ref):
+def away_kernel(plane_ref, weight_ref, first_ref, late_next_ref, early_next_ref):
+    odd, _, _ = position()
+    out_rows = first_ref.shape[0]
+    second = plane_taps(plane_ref[...], weight_ref, 2 - 2 * odd)
+    late_next_ref[...] = first_ref[...] + second
+    early_next_ref[:out_rows] = first_ref[...]
+    early_next_ref[out_rows:] = second
+
+
+def across_kernel(plane_ref, weight_ref, first_ref, pair_ref):
+    odd, _, _ = position()
+    out_rows = first_ref.shape[0]
+    second = plane_taps(plane_ref[...], weight_ref, 2 * odd)
+    pair_ref[:out_rows] = first_ref[...] + shared(second)
+    pair_ref[out_rows:] = second
+
+
+def centre_kernel(plane_ref, second_ref, own_ref, other_ref, pair_ref, centre_ref):
+    odd, _, _ = position()
     out_rows = centre_ref.shape[0] // 2
+    pair = pair_ref[1 - odd]
+    first = plane_taps(plane_ref[...], own_ref, 1)
     second = plane_taps(second_ref[...], other_ref, 1)
-    centre_ref[:out_rows] = plane_taps(plane_ref[...], own_ref, 1) + shared(second)
-    centre_ref[out_rows:] = second
+    centre_ref[:out_rows] = first + shared(second) + pair[:out_rows]
+    centre_ref[out_rows:] = second + pair[out_rows:]
 
 
 def sums(body, out_rows, *args):
@@ -212,15 +215,16 @@
     own, other = picks(late_kernel, own_in, kernel, early_own, received)
 
     first = sums(first_kernel, (own_out, own_out), plane, own)
-    late_to_next, early_to_next, to_pair = sums(
-        second_kernel, (own_out, 2 * own_out, 2 * own_out), second, other, *first
+    late_to_next, early_to_next = sums(
+        away_kernel, (own_out, 2 * own_out), second, other, first[0]
     )
+    (to_pair,) = sums(across_kernel, (2 * own_out,), second, other, first[1])
     both_axes = ("slab", "filt")
     early_from_next = lax.ppermute(early_to_next, both_axes, crossing(early))
     late_from_next = lax.ppermute(late_to_next, both_axes, crossing([not e for e in early]))
     from_pair = lax.all_gather(to_pair, "slab", axis=0, axis_index_groups=pairs)
-    (centre,) = sums(centre_kernel, (2 * own_out,), plane, second, own, other)
-    own_sum, other_sum = added(centre, from_pair, late_from_next, early_from_next)
+    (centre,) = sums(centre_kernel, (2 * own_out,), plane, second, own, other, from_pair)
+    own_sum, other_sum = added(centre, late_from_next, early_from_next)
     from_other = lax.ppermute(other_sum, "filt", swap_early)
     summed = own_sum + from_other + channel_bias[:, None]
     return summed.reshape(own_out, planes, cells).astype(jnp.bfloat16)

time: 53.5 us -> 53.1 us (level)
    pallas_call x3 -> x4, Pallas kernels: 2.47 us -> 2.69 us  [sums(): pl.pallas_call(body, out_shape=tuple((jax.ShapeDtypeStruct((rows, cells),...]
  transfers between devices with their start and end apart: 5 -> 5, of which waited for: 2 -> 2; matrix products, arithmetic and copies ran while one was open for 0% -> 0% of each run, Pallas kernels for 3% -> 4%
where the time goes in v8:
time: 53.1 us; the launch traced here: 52.5 us
  blocking collectives  30.1 us (57%)
  starting transfers between devices  10.9 us (21%)
  waiting for transfers between devices  5.92 us (11%)
  Pallas kernels  4.68 us (9%)
  other arithmetic  0.71 us (1%)
    all_gather x1, blocking collectives, on_device(): lax.all_gather(both, 'filt', axis=0, tiled=True, axis_index_groups=alike)  17.2 us
    all_gather x1, blocking collectives, on_device(): lax.all_gather(block, 'filt', axis=0, tiled=True, axis_index_groups=rings)  9.55 us
    ppermute x1, starting transfers between devices, on_device(): received = lax.ppermute(for_partner, 'filt', swap_early)  4.28 us
    ppermute x1, waiting for transfers between devices, on_device(): from_other = lax.ppermute(other_sum, 'filt', swap_early)  3.49 us
    all_gather x1, blocking collectives, on_device(): from_pair = lax.all_gather(to_pair, 'slab', axis=0, axis_index_groups=pairs)  3.4 us
    ppermute x1, starting transfers between devices, on_device(): from_other = lax.ppermute(other_sum, 'filt', swap_early)  3.37 us
    pallas_call x4, Pallas kernels, sums(): pl.pallas_call(body, out_shape=tuple((jax.ShapeDtypeStruct((rows, cells),...  2.69 us
    ppermute x1, waiting for transfers between devices, on_device(): early_from_next = lax.ppermute(early_to_next, both_axes, crossing(early))  2.42 us
  transfers between devices with their start and end apart: 5, of which 2 were waited for; matrix products, arithmetic and copies ran while one was open for 0% of the time, Pallas kernels for 4%

profile of v8, /device:TPU:56, one launch (start us, length us, event | category | flops | bytes accessed | tf_op | source)
XLA Modules:
  0.0 52.5 jit_solution(11356579696798282437)
XLA Ops:
  0.0 0.0 copy-start
  0.0 1.9 %shard_map.37 = (bf16[864,256]{1,0:T(8,128)(2,1)S(1)}, bf16[864,256]{1,0:T(8,128)(2,1)S(1)}) custom-call(bf16[27,32,512]{2,1,0:T(8,128)(2,1)} %weight_ref.3), custom_call_target="tpu_custom_call" | custom-call | tf_op jit(solution)/shard_map/pallas_call | solution.py:86
  1.9 4.3 %collective-permute-start.1 = (bf16[864,256]{1,0:T(8,128)(2,1)S(1)}, bf16[864,256]{1,0:T(8,128)(2,1)S(1)}, u32[]{:S(2)}, u32[]{:S(2)}) collective-permute-start(bf16[864,256]{1,0:T(8,128)(2,1)S(1)} %get-tuple-element.16), channel_id=1, source_target_pairs={{0,1},{1,0},{2,3},{3,2},{8,9},{9,8},{10,11},{11,10},{16,17},{17,16... | collective-permute-start | bytes 1327112 | tf_op jit(solution)/shard_map/ppermute | solution.py:210
  6.2 0.0 copy-done
  6.2 9.6 %all-gather = bf16[64,1,1024]{2,0,1:T(8,128)(2,1)S(1)} all-gather(bf16[32,1,1024]{2,0,1:T(8,128)(2,1)S(1)} %copy-done), channel_id=2, replica_groups={{0,8},{1,9},{2,10},{3,11},{4,12},{5,13},{6,14},{7,15},{16,24},{17,25},{..., dimensions={0}, use_global_device_ids=true | all-gather | bytes 196608 | tf_op jit(solution)/shard_map/all_gather | solution.py:212
  15.7 17.2 %all-gather.1 = bf16[256,1,1024]{2,0,1:T(8,128)(2,1)S(1)} all-gather(bf16[64,1,1024]{2,0,1:T(8,128)(2,1)S(1)} %all-gather), channel_id=3, replica_groups={{0,2,4,6},{1,3,5,7},{8,10,12,14},{9,11,13,15},{16,18,20,22},{17,19,21,2..., dimensions={0}, use_global_device_ids=true | all-gather | bytes 655360 | tf_op jit(solution)/shard_map/all_gather | solution.py:213
  32.9 0.7 %collective-permute-start = (bf16[256,1024]{1,0:T(8,128)(2,1)S(1)}, bf16[256,1024]{1,0:T(8,128)(2,1)S(1)}, u32[]{:S(2)}, u32[]{:S(2)}) collective-permute-start(bf16[256,1024]{1,0:T(8,128)(2,1)S(1)} %bitcast.4), channel_id=1, source_target_pairs={{0,0},{1,1},{2,2},{3,3},{8,8},{9,9},{10,10},{11,11},{4,5},{5,4},{6... | collective-permute-start | bytes 1572872 | tf_op jit(solution)/shard_map/ppermute | solution.py:214
  33.6 0.0 collective-permute-done.1.received_ref
  33.6 0.1 shard_map.38
  33.7 0.8 %shard_map.39 = (f32[32,1024]{1,0:T(8,128)S(1)}, f32[32,1024]{1,0:T(8,128)S(1)}) custom-call(bf16[256,1024]{1,0:T(8,128)(2,1)S(1)} %bitcast.5, bf16[864,256]{1,0:T(8,128)(2,1)S(1)} %get-tuple-element.17.weight_ref.own_ref), custom_call_target="tpu_custom_call" | custom-call | tf_op jit(solution)/shard_map/pallas_call | solution.py:172
  34.5 0.0 collective-permute-done.plane_ref.second_ref
  34.5 0.5 %shard_map.42 = (f32[32,1024]{1,0:T(8,128)S(1)}, f32[64,1024]{1,0:T(8,128)S(1)}) custom-call(bf16[256,1024]{1,0:T(8,128)(2,1)S(1)} %collective-permute-done.plane_ref.second_ref, bf16[864,256]{1,0:T(8,128)(2,1)S(1)} %get-tuple-element.18.weight_ref.other_ref, f32[32,1024]{1,0:T(8,128)S(1)} %get-tuple-element.20.first_ref), custom_call_target="tpu_custom_call" | custom-call | tf_op jit(solution)/shard_map/pallas_call | solution.py:172
  35.1 1.9 %collective-permute-start.3 = (f32[64,1024]{1,0:T(8,128)S(1)}, f32[64,1024]{1,0:T(8,128)S(1)}, u32[]{:S(2)}, u32[]{:S(2)}) collective-permute-start(f32[64,1024]{1,0:T(8,128)S(1)} %get-tuple-element.22), channel_id=1, source_target_pairs={{16,32},{17,33},{18,34},{19,35},{24,40},{25,41},{26,42},{27,43},{4... | collective-permute-start | bytes 786440 | tf_op jit(solution)/shard_map/ppermute | solution.py:223
  37.0 0.7 %collective-permute-start.2 = (f32[32,1024]{1,0:T(8,128)S(1)}, f32[32,1024]{1,0:T(8,128)S(1)}, u32[]{:S(2)}, u32[]{:S(2)}) collective-permute-start(f32[32,1024]{1,0:T(8,128)S(1)} %get-tuple-element.21), channel_id=1, source_target_pairs={{20,36},{21,37},{22,38},{23,39},{28,44},{29,45},{30,46},{31,47},{5... | collective-permute-start | bytes 393224 | tf_op jit(solution)/shard_map/ppermute | solution.py:224
  37.7 0.5 %shard_map.40 = f32[64,1024]{1,0:T(8,128)S(1)} custom-call(bf16[256,1024]{1,0:T(8,128)(2,1)S(1)} %collective-permute-done.plane_ref.second_ref, bf16[864,256]{1,0:T(8,128)(2,1)S(1)} %get-tuple-element.18.weight_ref.other_ref, f32[32,1024]{1,0:T(8,128)S(1)} %get-tuple-element.19.first_ref), custom_call_target="tpu_custom_call" | custom-call | tf_op jit(solution)/shard_map/pallas_call | solution.py:172
  38.2 3.4 %all-gather.2 = f32[128,1024]{1,0:T(8,128)S(1)} all-gather(f32[64,1024]{1,0:T(8,128)S(1)} %shard_map.40), channel_id=4, replica_groups={{0,16},{32,48},{64,80},{96,112},{128,144},{160,176},{192,208},{224,240}..., dimensions={0}, use_global_device_ids=true | all-gather | bytes 786432 | tf_op jit(solution)/shard_map/all_gather | solution.py:225
  41.6 0.8 %shard_map.41.centre_ref = f32[64,1024]{1,0:T(8,128)S(1)} custom-call(bf16[256,1024]{1,0:T(8,128)(2,1)S(1)} %bitcast.6, bf16[256,1024]{1,0:T(8,128)(2,1)S(1)} %collective-permute-done.plane_ref.second_ref, bf16[864,256]{1,0:T(8,128)(2,1)S(1)} %get-tuple-element.17.weight_ref.own_ref, bf16[864,256]{1,0:T(8,128)(2,1)S(1)} %get-tuple-element.18.weight_ref.other_ref, ...), custom_call_target="tpu_custom_call" | custom-call | tf_op jit(solution)/shard_map/pallas_call | solution.py:172
  42.4 0.0 collective-permute-done.2.late_next_ref
  42.4 2.4 %collective-permute-done.3.early_next_ref = f32[64,1024]{1,0:T(8,128)S(1)} collective-permute-done((f32[64,1024]{1,0:T(8,128)S(1)}, f32[64,1024]{1,0:T(8,128)S(1)}, u32[]{:S(2)}, u32[]{:S(2)}) %collective-permute-start.3) | collective-permute-done | bytes 262176 | tf_op jit(solution)/shard_map/ppermute | solution.py:223
  44.9 0.0 copy-start.1
  44.9 3.4 %collective-permute-start.4 = (f32[32,1024]{1,0:T(8,128)S(1)}, f32[32,1024]{1,0:T(8,128)S(1)}, u32[]{:S(2)}, u32[]{:S(2)}) collective-permute-start(f32[32,1024]{1,0:T(8,128)S(1)} %get-tuple-element.24), channel_id=1, source_target_pairs={{0,1},{1,0},{2,3},{3,2},{8,9},{9,8},{10,11},{11,10},{16,17},{17,16... | collective-permute-start | bytes 393224 | tf_op jit(solution)/shard_map/ppermute | solution.py:228
  48.3 3.5 %collective-permute-done.4 = f32[32,1024]{1,0:T(8,128)S(1)} collective-permute-done((f32[32,1024]{1,0:T(8,128)S(1)}, f32[32,1024]{1,0:T(8,128)S(1)}, u32[]{:S(2)}, u32[]{:S(2)}) %collective-permute-start.4) | collective-permute-done | bytes 131104 | tf_op jit(solution)/shard_map/ppermute | solution.py:228
  51.8 0.0 copy-done.1
  51.8 0.7 %fusion = bf16[32,1,1024]{2,0,1:T(8,128)(2,1)} fusion(f32[32,1024]{1,0:T(8,128)S(1)} %get-tuple-element.23, f32[32,1024]{1,0:T(8,128)S(1)} %collective-permute-done.4, f32[32]{0:T(128)S(1)} %copy-done.1), kind=kLoop, calls=%fused_computation.1 | loop fusion | flops 98304 | bytes 327808 | tf_op jit(solution)/shard_map/convert_element_type | solution.py:230
  (1 shorter events, 0.0 us)
Async XLA Ops:
  0.0 6.2 %copy-start = (bf16[32,1,1024]{2,0,1:T(8,128)(2,1)S(1)}, bf16[32,1,1024]{2,0,1:T(8,128)(2,1)}, u32[]{:S(2)}) copy-start(bf16[32,1,1024]{2,0,1:T(8,128)(2,1)} %param.3) | copy-start | bytes 196612
  1.9 31.7 %collective-permute-start.1 = (bf16[864,256]{1,0:T(8,128)(2,1)S(1)}, bf16[864,256]{1,0:T(8,128)(2,1)S(1)}, u32[]{:S(2)}, u32[]{:S(2)}) collective-permute-start(bf16[864,256]{1,0:T(8,128)(2,1)S(1)} %get-tuple-element.16), channel_id=1, source_target_pairs={{0,1},{1,0},{2,3},{3,2},{8,9},{9,8},{10,11},{11,10},{16,17},{17,16... | collective-permute-start | bytes 1327112 | tf_op jit(solution)/shard_map/ppermute | solution.py:210
  32.9 1.6 %collective-permute-start = (bf16[256,1024]{1,0:T(8,128)(2,1)S(1)}, bf16[256,1024]{1,0:T(8,128)(2,1)S(1)}, u32[]{:S(2)}, u32[]{:S(2)}) collective-permute-start(bf16[256,1024]{1,0:T(8,128)(2,1)S(1)} %bitcast.4), channel_id=1, source_target_pairs={{0,0},{1,1},{2,2},{3,3},{8,8},{9,9},{10,10},{11,11},{4,5},{5,4},{6... | collective-permute-start | bytes 1572872 | tf_op jit(solution)/shard_map/ppermute | solution.py:214
  35.1 9.8 %collective-permute-start.3 = (f32[64,1024]{1,0:T(8,128)S(1)}, f32[64,1024]{1,0:T(8,128)S(1)}, u32[]{:S(2)}, u32[]{:S(2)}) collective-permute-start(f32[64,1024]{1,0:T(8,128)S(1)} %get-tuple-element.22), channel_id=1, source_target_pairs={{16,32},{17,33},{18,34},{19,35},{24,40},{25,41},{26,42},{27,43},{4... | collective-permute-start | bytes 786440 | tf_op jit(solution)/shard_map/ppermute | solution.py:223
  37.0 5.4 %collective-permute-start.2 = (f32[32,1024]{1,0:T(8,128)S(1)}, f32[32,1024]{1,0:T(8,128)S(1)}, u32[]{:S(2)}, u32[]{:S(2)}) collective-permute-start(f32[32,1024]{1,0:T(8,128)S(1)} %get-tuple-element.21), channel_id=1, source_target_pairs={{20,36},{21,37},{22,38},{23,39},{28,44},{29,45},{30,46},{31,47},{5... | collective-permute-start | bytes 393224 | tf_op jit(solution)/shard_map/ppermute | solution.py:224
  44.9 6.9 %copy-start.1 = (f32[32]{0:T(128)S(1)}, f32[32]{0:T(128)}, u32[]{:S(2)}) copy-start(f32[32]{0:T(128)} %param.5) | copy-start | bytes 388
  44.9 6.9 %collective-permute-start.4 = (f32[32,1024]{1,0:T(8,128)S(1)}, f32[32,1024]{1,0:T(8,128)S(1)}, u32[]{:S(2)}, u32[]{:S(2)}) collective-permute-start(f32[32,1024]{1,0:T(8,128)S(1)} %get-tuple-element.24), channel_id=1, source_target_pairs={{0,1},{1,0},{2,3},{3,2},{8,9},{9,8},{10,11},{11,10},{16,17},{17,16... | collective-permute-start | bytes 393224 | tf_op jit(solution)/shard_map/ppermute | solution.py:228

commit v9 on v8

--- a/solution.py
+++ b/solution.py
@@ -94,22 +94,21 @@
     )(pltpu.with_memory_space_constraint(weights, pltpu.HBM), *early)
 
 
-def add_kernel(centre_ref, late_next_ref, early_next_ref, own_ref, other_ref):
+def add_kernel(centre_ref, early_next_ref, own_ref, other_ref):
     out_rows = own_ref.shape[0]
-    total = centre_ref[...] + early_next_ref[...]
-    other_ref[...] = total[out_rows:]
-    own_ref[...] = total[:out_rows] + late_next_ref[...]
-
-
-def added(centre, *parts):
+    other_ref[...] = centre_ref[out_rows:] + early_next_ref[out_rows:]
+    own_ref[...] = centre_ref[:out_rows] + early_next_ref[:out_rows]
+
+
+def added(centre, early_next):
     half = jax.ShapeDtypeStruct((centre.shape[0] // 2, centre.shape[1]), centre.dtype)
     return pl.pallas_call(
         add_kernel,
         out_shape=(half, half),
-        in_specs=[VMEM] * (1 + len(parts)),
+        in_specs=[VMEM] * 2,
         out_specs=(VMEM,) * 2,
         compiler_params=PARAMS,
-    )(centre, *parts)
+    )(centre, early_next)
 
 
 def in_plane(product):
@@ -128,11 +127,9 @@
     return in_plane(jnp.dot(group, plane, preferred_element_type=jnp.float32))
 
 
-def first_kernel(plane_ref, weight_ref, next_ref, pair_ref):
-    plane = plane_ref[...]
-    odd, _, _ = position()
-    next_ref[...] = plane_taps(plane, weight_ref, 2 - 2 * odd)
-    pair_ref[...] = plane_taps(plane, weight_ref, 2 * odd)
+def first_kernel(plane_ref, weight_ref, next_ref):
+    odd, _, _ = position()
+    next_ref[...] = plane_taps(plane_ref[...], weight_ref, 2 - 2 * odd)
 
 
 def shared(second):
@@ -149,11 +146,11 @@
     early_next_ref[out_rows:] = second
 
 
-def across_kernel(plane_ref, weight_ref, first_ref, pair_ref):
-    odd, _, _ = position()
-    out_rows = first_ref.shape[0]
-    second = plane_taps(plane_ref[...], weight_ref, 2 * odd)
-    pair_ref[:out_rows] = first_ref[...] + shared(second)
+def across_kernel(plane_ref, second_ref, own_ref, other_ref, pair_ref):
+    odd, _, _ = position()
+    out_rows = pair_ref.shape[0] // 2
+    second = plane_taps(second_ref[...], other_ref, 2 * odd)
+    pair_ref[:out_rows] = plane_taps(plane_ref[...], own_ref, 2 * odd) + shared(second)
     pair_ref[out_rows:] = second
 
 
@@ -214,19 +211,19 @@
     second = lax.ppermute(plane, "filt", keep_early + swap_late)
     own, other = picks(late_kernel, own_in, kernel, early_own, received)
 
-    first = sums(first_kernel, (own_out, own_out), plane, own)
+    (first,) = sums(first_kernel, (own_out,), plane, own)
     late_to_next, early_to_next = sums(
-        away_kernel, (own_out, 2 * own_out), second, other, first[0]
+        away_kernel, (own_out, 2 * own_out), second, other, first
     )
-    (to_pair,) = sums(across_kernel, (2 * own_out,), second, other, first[1])
+    (to_pair,) = sums(across_kernel, (2 * own_out,), plane, second, own, other)
     both_axes = ("slab", "filt")
     early_from_next = lax.ppermute(early_to_next, both_axes, crossing(early))
     late_from_next = lax.ppermute(late_to_next, both_axes, crossing([not e for e in early]))
     from_pair = lax.all_gather(to_pair, "slab", axis=0, axis_index_groups=pairs)
     (centre,) = sums(centre_kernel, (2 * own_out,), plane, second, own, other, from_pair)
-    own_sum, other_sum = added(centre, late_from_next, early_from_next)
+    own_sum, other_sum = added(centre, early_from_next)
     from_other = lax.ppermute(other_sum, "filt", swap_early)
-    summed = own_sum + from_other + channel_bias[:, None]
+    summed = own_sum + late_from_next + from_other + channel_bias[:, None]
     return summed.reshape(own_out, planes, cells).astype(jnp.bfloat16)
 
 

time: 53.1 us -> 52.4 us (0.987)
  no operation moved by 1% of the time
where the time goes in v9:
time: 52.4 us; the launch traced here: 52.2 us
  blocking collectives  30.1 us (57%)
  starting transfers between devices  10.9 us (21%)
  waiting for transfers between devices  5.64 us (11%)
  Pallas kernels  4.69 us (9%)
  other arithmetic  0.71 us (1%)
    all_gather x1, blocking collectives, on_device(): lax.all_gather(both, 'filt', axis=0, tiled=True, axis_index_groups=alike)  17.2 us
    all_gather x1, blocking collectives, on_device(): lax.all_gather(block, 'filt', axis=0, tiled=True, axis_index_groups=rings)  9.55 us
    ppermute x1, starting transfers between devices, on_device(): received = lax.ppermute(for_partner, 'filt', swap_early)  4.28 us
    ppermute x1, waiting for transfers between devices, on_device(): from_other = lax.ppermute(other_sum, 'filt', swap_early)  3.49 us
    all_gather x1, blocking collectives, on_device(): from_pair = lax.all_gather(to_pair, 'slab', axis=0, axis_index_groups=pairs)  3.4 us
    ppermute x1, starting transfers between devices, on_device(): from_other = lax.ppermute(other_sum, 'filt', swap_early)  3.35 us
    pallas_call x4, Pallas kernels, sums(): pl.pallas_call(body, out_shape=tuple((jax.ShapeDtypeStruct((rows, cells),...  2.71 us
    ppermute x1, waiting for transfers between devices, on_device(): early_from_next = lax.ppermute(early_to_next, both_axes, crossing(early))  2.14 us
  transfers between devices with their start and end apart: 5, of which 2 were waited for; matrix products, arithmetic and copies ran while one was open for 0% of the time, Pallas kernels for 4%

profile of v9, /device:TPU:56, one launch (start us, length us, event | category | flops | bytes accessed | tf_op | source)
XLA Modules:
  0.0 52.2 jit_solution(15175285745442150513)
XLA Ops:
  0.0 0.0 copy-start
  0.0 1.9 %shard_map.37 = (bf16[864,256]{1,0:T(8,128)(2,1)S(1)}, bf16[864,256]{1,0:T(8,128)(2,1)S(1)}) custom-call(bf16[27,32,512]{2,1,0:T(8,128)(2,1)} %weight_ref.3), custom_call_target="tpu_custom_call" | custom-call | tf_op jit(solution)/shard_map/pallas_call | solution.py:86
  1.9 4.3 %collective-permute-start.1 = (bf16[864,256]{1,0:T(8,128)(2,1)S(1)}, bf16[864,256]{1,0:T(8,128)(2,1)S(1)}, u32[]{:S(2)}, u32[]{:S(2)}) collective-permute-start(bf16[864,256]{1,0:T(8,128)(2,1)S(1)} %get-tuple-element.14), channel_id=1, source_target_pairs={{0,1},{1,0},{2,3},{3,2},{8,9},{9,8},{10,11},{11,10},{16,17},{17,16... | collective-permute-start | bytes 1327112 | tf_op jit(solution)/shard_map/ppermute | solution.py:207
  6.2 0.0 copy-done
  6.2 9.6 %all-gather = bf16[64,1,1024]{2,0,1:T(8,128)(2,1)S(1)} all-gather(bf16[32,1,1024]{2,0,1:T(8,128)(2,1)S(1)} %copy-done), channel_id=2, replica_groups={{0,8},{1,9},{2,10},{3,11},{4,12},{5,13},{6,14},{7,15},{16,24},{17,25},{..., dimensions={0}, use_global_device_ids=true | all-gather | bytes 196608 | tf_op jit(solution)/shard_map/all_gather | solution.py:209
  15.7 17.2 %all-gather.1 = bf16[256,1,1024]{2,0,1:T(8,128)(2,1)S(1)} all-gather(bf16[64,1,1024]{2,0,1:T(8,128)(2,1)S(1)} %all-gather), channel_id=3, replica_groups={{0,2,4,6},{1,3,5,7},{8,10,12,14},{9,11,13,15},{16,18,20,22},{17,19,21,2..., dimensions={0}, use_global_device_ids=true | all-gather | bytes 655360 | tf_op jit(solution)/shard_map/all_gather | solution.py:210
  32.9 0.7 %collective-permute-start = (bf16[256,1024]{1,0:T(8,128)(2,1)S(1)}, bf16[256,1024]{1,0:T(8,128)(2,1)S(1)}, u32[]{:S(2)}, u32[]{:S(2)}) collective-permute-start(bf16[256,1024]{1,0:T(8,128)(2,1)S(1)} %bitcast.4), channel_id=1, source_target_pairs={{0,0},{1,1},{2,2},{3,3},{8,8},{9,9},{10,10},{11,11},{4,5},{5,4},{6... | collective-permute-start | bytes 1572872 | tf_op jit(solution)/shard_map/ppermute | solution.py:211
  33.6 0.0 collective-permute-done.1.received_ref
  33.6 0.1 shard_map.38
  33.7 0.5 %shard_map.41.first_ref = f32[32,1024]{1,0:T(8,128)S(1)} custom-call(bf16[256,1024]{1,0:T(8,128)(2,1)S(1)} %bitcast.5, bf16[864,256]{1,0:T(8,128)(2,1)S(1)} %get-tuple-element.15.own_ref.weight_ref), custom_call_target="tpu_custom_call" | custom-call | tf_op jit(solution)/shard_map/pallas_call | solution.py:169
  34.2 0.0 collective-permute-done.second_ref.plane_ref
  34.2 0.5 %shard_map.42 = (f32[32,1024]{1,0:T(8,128)S(1)}, f32[64,1024]{1,0:T(8,128)S(1)}) custom-call(bf16[256,1024]{1,0:T(8,128)(2,1)S(1)} %collective-permute-done.second_ref.plane_ref, bf16[864,256]{1,0:T(8,128)(2,1)S(1)} %get-tuple-element.16.other_ref.weight_ref, f32[32,1024]{1,0:T(8,128)S(1)} %shard_map.41.first_ref), custom_call_target="tpu_custom_call" | custom-call | tf_op jit(solution)/shard_map/pallas_call | solution.py:169
  34.8 1.9 %collective-permute-start.2 = (f32[64,1024]{1,0:T(8,128)S(1)}, f32[64,1024]{1,0:T(8,128)S(1)}, u32[]{:S(2)}, u32[]{:S(2)}) collective-permute-start(f32[64,1024]{1,0:T(8,128)S(1)} %get-tuple-element.17), channel_id=1, source_target_pairs={{16,32},{17,33},{18,34},{19,35},{24,40},{25,41},{26,42},{27,43},{4... | collective-permute-start | bytes 786440 | tf_op jit(solution)/shard_map/ppermute | solution.py:220
  36.7 0.7 %collective-permute-start.3 = (f32[32,1024]{1,0:T(8,128)S(1)}, f32[32,1024]{1,0:T(8,128)S(1)}, u32[]{:S(2)}, u32[]{:S(2)}) collective-permute-start(f32[32,1024]{1,0:T(8,128)S(1)} %get-tuple-element.19), channel_id=1, source_target_pairs={{20,36},{21,37},{22,38},{23,39},{28,44},{29,45},{30,46},{31,47},{5... | collective-permute-start | bytes 393224 | tf_op jit(solution)/shard_map/ppermute | solution.py:221
  37.4 0.8 %shard_map.39 = f32[64,1024]{1,0:T(8,128)S(1)} custom-call(bf16[256,1024]{1,0:T(8,128)(2,1)S(1)} %bitcast.6, bf16[256,1024]{1,0:T(8,128)(2,1)S(1)} %collective-permute-done.second_ref.plane_ref, bf16[864,256]{1,0:T(8,128)(2,1)S(1)} %get-tuple-element.15.own_ref.weight_ref, bf16[864,256]{1,0:T(8,128)(2,1)S(1)} %get-tuple-element.16.other_ref.weight_ref), custom_call_target="tpu_custom_call" | custom-call | tf_op jit(solution)/shard_map/pallas_call | solution.py:169
  38.2 3.4 %all-gather.2 = f32[128,1024]{1,0:T(8,128)S(1)} all-gather(f32[64,1024]{1,0:T(8,128)S(1)} %shard_map.39), channel_id=4, replica_groups={{0,16},{32,48},{64,80},{96,112},{128,144},{160,176},{192,208},{224,240}..., dimensions={0}, use_global_device_ids=true | all-gather | bytes 786432 | tf_op jit(solution)/shard_map/all_gather | solution.py:222
  41.6 0.8 %shard_map.40.centre_ref = f32[64,1024]{1,0:T(8,128)S(1)} custom-call(bf16[256,1024]{1,0:T(8,128)(2,1)S(1)} %bitcast.7, bf16[256,1024]{1,0:T(8,128)(2,1)S(1)} %collective-permute-done.second_ref.plane_ref, bf16[864,256]{1,0:T(8,128)(2,1)S(1)} %get-tuple-element.15.own_ref.weight_ref, bf16[864,256]{1,0:T(8,128)(2,1)S(1)} %get-tuple-element.16.other_ref.weight_ref, ...), custom_call_target="tpu_custom_call" | custom-call | tf_op jit(solution)/shard_map/pallas_call | solution.py:169
  42.4 2.1 %collective-permute-done.2.early_next_ref = f32[64,1024]{1,0:T(8,128)S(1)} collective-permute-done((f32[64,1024]{1,0:T(8,128)S(1)}, f32[64,1024]{1,0:T(8,128)S(1)}, u32[]{:S(2)}, u32[]{:S(2)}) %collective-permute-start.2) | collective-permute-done | bytes 262176 | tf_op jit(solution)/shard_map/ppermute | solution.py:220
  44.6 0.0 copy-start.1
  44.6 3.3 %collective-permute-start.4 = (f32[32,1024]{1,0:T(8,128)S(1)}, f32[32,1024]{1,0:T(8,128)S(1)}, u32[]{:S(2)}, u32[]{:S(2)}) collective-permute-start(f32[32,1024]{1,0:T(8,128)S(1)} %get-tuple-element.20), channel_id=1, source_target_pairs={{0,1},{1,0},{2,3},{3,2},{8,9},{9,8},{10,11},{11,10},{16,17},{17,16... | collective-permute-start | bytes 393224 | tf_op jit(solution)/shard_map/ppermute | solution.py:225
  48.0 0.0 collective-permute-done.3
  48.0 3.5 %collective-permute-done.4 = f32[32,1024]{1,0:T(8,128)S(1)} collective-permute-done((f32[32,1024]{1,0:T(8,128)S(1)}, f32[32,1024]{1,0:T(8,128)S(1)}, u32[]{:S(2)}, u32[]{:S(2)}) %collective-permute-start.4) | collective-permute-done | bytes 131104 | tf_op jit(solution)/shard_map/ppermute | solution.py:225
  51.5 0.0 copy-done.1
  51.5 0.7 %fusion = bf16[32,1,1024]{2,0,1:T(8,128)(2,1)} fusion(f32[32,1024]{1,0:T(8,128)S(1)} %collective-permute-done.4, f32[32,1024]{1,0:T(8,128)S(1)} %get-tuple-element.18, f32[32,1024]{1,0:T(8,128)S(1)} %collective-permute-done.3, f32[32]{0:T(128)S(1)} %copy-done.1), kind=kLoop, calls=%fused_computation.1 | loop fusion | flops 131072 | bytes 458880 | tf_op jit(solution)/shard_map/convert_element_type | solution.py:227
  (1 shorter events, 0.0 us)
Async XLA Ops:
  0.0 6.2 %copy-start = (bf16[32,1,1024]{2,0,1:T(8,128)(2,1)S(1)}, bf16[32,1,1024]{2,0,1:T(8,128)(2,1)}, u32[]{:S(2)}) copy-start(bf16[32,1,1024]{2,0,1:T(8,128)(2,1)} %param.3) | copy-start | bytes 196612
  1.9 31.7 %collective-permute-start.1 = (bf16[864,256]{1,0:T(8,128)(2,1)S(1)}, bf16[864,256]{1,0:T(8,128)(2,1)S(1)}, u32[]{:S(2)}, u32[]{:S(2)}) collective-permute-start(bf16[864,256]{1,0:T(8,128)(2,1)S(1)} %get-tuple-element.14), channel_id=1, source_target_pairs={{0,1},{1,0},{2,3},{3,2},{8,9},{9,8},{10,11},{11,10},{16,17},{17,16... | collective-permute-start | bytes 1327112 | tf_op jit(solution)/shard_map/ppermute | solution.py:207
  32.9 1.3 %collective-permute-start = (bf16[256,1024]{1,0:T(8,128)(2,1)S(1)}, bf16[256,1024]{1,0:T(8,128)(2,1)S(1)}, u32[]{:S(2)}, u32[]{:S(2)}) collective-permute-start(bf16[256,1024]{1,0:T(8,128)(2,1)S(1)} %bitcast.4), channel_id=1, source_target_pairs={{0,0},{1,1},{2,2},{3,3},{8,8},{9,9},{10,10},{11,11},{4,5},{5,4},{6... | collective-permute-start | bytes 1572872 | tf_op jit(solution)/shard_map/ppermute | solution.py:211
  34.8 9.8 %collective-permute-start.2 = (f32[64,1024]{1,0:T(8,128)S(1)}, f32[64,1024]{1,0:T(8,128)S(1)}, u32[]{:S(2)}, u32[]{:S(2)}) collective-permute-start(f32[64,1024]{1,0:T(8,128)S(1)} %get-tuple-element.17), channel_id=1, source_target_pairs={{16,32},{17,33},{18,34},{19,35},{24,40},{25,41},{26,42},{27,43},{4... | collective-permute-start | bytes 786440 | tf_op jit(solution)/shard_map/ppermute | solution.py:220
  36.7 11.3 %collective-permute-start.3 = (f32[32,1024]{1,0:T(8,128)S(1)}, f32[32,1024]{1,0:T(8,128)S(1)}, u32[]{:S(2)}, u32[]{:S(2)}) collective-permute-start(f32[32,1024]{1,0:T(8,128)S(1)} %get-tuple-element.19), channel_id=1, source_target_pairs={{20,36},{21,37},{22,38},{23,39},{28,44},{29,45},{30,46},{31,47},{5... | collective-permute-start | bytes 393224 | tf_op jit(solution)/shard_map/ppermute | solution.py:221
  44.6 6.9 %copy-start.1 = (f32[32]{0:T(128)S(1)}, f32[32]{0:T(128)}, u32[]{:S(2)}) copy-start(f32[32]{0:T(128)} %param.5) | copy-start | bytes 388
  44.6 6.9 %collective-permute-start.4 = (f32[32,1024]{1,0:T(8,128)S(1)}, f32[32,1024]{1,0:T(8,128)S(1)}, u32[]{:S(2)}, u32[]{:S(2)}) collective-permute-start(f32[32,1024]{1,0:T(8,128)S(1)} %get-tuple-element.20), channel_id=1, source_target_pairs={{0,1},{1,0},{2,3},{3,2},{8,9},{9,8},{10,11},{11,10},{16,17},{17,16... | collective-permute-start | bytes 393224 | tf_op jit(solution)/shard_map/ppermute | solution.py:225

commit v10 on v9

--- a/solution.py
+++ b/solution.py
@@ -94,23 +94,6 @@
     )(pltpu.with_memory_space_constraint(weights, pltpu.HBM), *early)
 
 
-def add_kernel(centre_ref, early_next_ref, own_ref, other_ref):
-    out_rows = own_ref.shape[0]
-    other_ref[...] = centre_ref[out_rows:] + early_next_ref[out_rows:]
-    own_ref[...] = centre_ref[:out_rows] + early_next_ref[:out_rows]
-
-
-def added(centre, early_next):
-    half = jax.ShapeDtypeStruct((centre.shape[0] // 2, centre.shape[1]), centre.dtype)
-    return pl.pallas_call(
-        add_kernel,
-        out_shape=(half, half),
-        in_specs=[VMEM] * 2,
-        out_specs=(VMEM,) * 2,
-        compiler_params=PARAMS,
-    )(centre, early_next)
-
-
 def in_plane(product):
     rows = product.shape[0] // 9
     taps = [product[tap * rows : (tap + 1) * rows] for tap in range(9)]
@@ -154,14 +137,23 @@
     pair_ref[out_rows:] = second
 
 
-def centre_kernel(plane_ref, second_ref, own_ref, other_ref, pair_ref, centre_ref):
-    odd, _, _ = position()
-    out_rows = centre_ref.shape[0] // 2
-    pair = pair_ref[1 - odd]
-    first = plane_taps(plane_ref[...], own_ref, 1)
-    second = plane_taps(second_ref[...], other_ref, 1)
-    centre_ref[:out_rows] = first + shared(second) + pair[:out_rows]
-    centre_ref[out_rows:] = second + pair[out_rows:]
+def other_add_kernel(first_ref, next_ref, sum_ref):
+    sum_ref[...] = first_ref[...] + next_ref[first_ref.shape[0] :]
+
+
+def other_centre_kernel(second_ref, weight_ref, pair_ref, centre_ref, sum_ref):
+    odd, _, _ = position()
+    out_rows = sum_ref.shape[0]
+    centre = plane_taps(second_ref[...], weight_ref, 1)
+    centre_ref[...] = centre
+    sum_ref[...] = centre + pair_ref[1 - odd, out_rows:]
+
+
+def own_centre_kernel(plane_ref, weight_ref, pair_ref, next_ref, second_ref, sum_ref):
+    odd, _, _ = position()
+    out_rows = sum_ref.shape[0]
+    centre = plane_taps(plane_ref[...], weight_ref, 1) + shared(second_ref[...])
+    sum_ref[...] = centre + pair_ref[1 - odd, :out_rows] + next_ref[:out_rows]
 
 
 def sums(body, out_rows, *args):
@@ -220,9 +212,13 @@
     early_from_next = lax.ppermute(early_to_next, both_axes, crossing(early))
     late_from_next = lax.ppermute(late_to_next, both_axes, crossing([not e for e in early]))
     from_pair = lax.all_gather(to_pair, "slab", axis=0, axis_index_groups=pairs)
-    (centre,) = sums(centre_kernel, (2 * own_out,), plane, second, own, other, from_pair)
-    own_sum, other_sum = added(centre, early_from_next)
+    halo = (from_pair, early_from_next)
+    centre, other_sum = sums(
+        other_centre_kernel, (own_out, own_out), second, other, from_pair
+    )
+    (other_sum,) = sums(other_add_kernel, (own_out,), other_sum, early_from_next)
     from_other = lax.ppermute(other_sum, "filt", swap_early)
+    (own_sum,) = sums(own_centre_kernel, (own_out,), plane, own, *halo, centre)
     summed = own_sum + late_from_next + from_other + channel_bias[:, None]
     return summed.reshape(own_out, planes, cells).astype(jnp.bfloat16)
 

time: 52.4 us -> 52.6 us (level)
    ppermute x1, waiting for transfers between devices: 3.49 us -> 2.94 us  [on_device(): from_other = lax.ppermute(other_sum, 'filt', swap_early)]
    pallas_call x4 -> x6, Pallas kernels: 2.71 us -> 2.98 us  [sums(): pl.pallas_call(body, out_shape=tuple((jax.ShapeDtypeStruct((rows, cells),...]
  transfers between devices with their start and end apart: 5 -> 5, of which waited for: 2 -> 2; matrix products, arithmetic and copies ran while one was open for 0% -> 0% of each run, Pallas kernels for 4% -> 5%
where the time goes in v10:
time: 52.6 us; the launch traced here: 52.2 us
  blocking collectives  30.1 us (57%)
  starting transfers between devices  10.9 us (21%)
  waiting for transfers between devices  5.37 us (10%)
  Pallas kernels  4.94 us (9%)
  other arithmetic  0.71 us (1%)
    all_gather x1, blocking collectives, on_device(): lax.all_gather(both, 'filt', axis=0, tiled=True, axis_index_groups=alike)  17.2 us
    all_gather x1, blocking collectives, on_device(): lax.all_gather(block, 'filt', axis=0, tiled=True, axis_index_groups=rings)  9.55 us
    ppermute x1, starting transfers between devices, on_device(): received = lax.ppermute(for_partner, 'filt', swap_early)  4.28 us
    all_gather x1, blocking collectives, on_device(): from_pair = lax.all_gather(to_pair, 'slab', axis=0, axis_index_groups=pairs)  3.4 us
    ppermute x1, starting transfers between devices, on_device(): from_other = lax.ppermute(other_sum, 'filt', swap_early)  3.35 us
    pallas_call x6, Pallas kernels, sums(): pl.pallas_call(body, out_shape=tuple((jax.ShapeDtypeStruct((rows, cells),...  2.98 us
    ppermute x1, waiting for transfers between devices, on_device(): from_other = lax.ppermute(other_sum, 'filt', swap_early)  2.94 us
    ppermute x1, waiting for transfers between devices, on_device(): early_from_next = lax.ppermute(early_to_next, both_axes, crossing(early))  2.42 us
  transfers between devices with their start and end apart: 5, of which 2 were waited for; matrix products, arithmetic and copies ran while one was open for 0% of the time, Pallas kernels for 5%

profile of v10, /device:TPU:56, one launch (start us, length us, event | category | flops | bytes accessed | tf_op | source)
XLA Modules:
  0.0 52.2 jit_solution(14173012069094042562)
XLA Ops:
  0.0 0.0 copy-start
  0.0 1.9 %shard_map.37 = (bf16[864,256]{1,0:T(8,128)(2,1)S(1)}, bf16[864,256]{1,0:T(8,128)(2,1)S(1)}) custom-call(bf16[27,32,512]{2,1,0:T(8,128)(2,1)} %weight_ref.3), custom_call_target="tpu_custom_call" | custom-call | tf_op jit(solution)/shard_map/pallas_call | solution.py:86
  1.9 4.3 %collective-permute-start = (bf16[864,256]{1,0:T(8,128)(2,1)S(1)}, bf16[864,256]{1,0:T(8,128)(2,1)S(1)}, u32[]{:S(2)}, u32[]{:S(2)}) collective-permute-start(bf16[864,256]{1,0:T(8,128)(2,1)S(1)} %get-tuple-element.14), channel_id=1, source_target_pairs={{0,1},{1,0},{2,3},{3,2},{8,9},{9,8},{10,11},{11,10},{16,17},{17,16... | collective-permute-start | bytes 1327112 | tf_op jit(solution)/shard_map/ppermute | solution.py:199
  6.2 0.0 copy-done
  6.2 9.6 %all-gather = bf16[64,1,1024]{2,0,1:T(8,128)(2,1)S(1)} all-gather(bf16[32,1,1024]{2,0,1:T(8,128)(2,1)S(1)} %copy-done), channel_id=2, replica_groups={{0,8},{1,9},{2,10},{3,11},{4,12},{5,13},{6,14},{7,15},{16,24},{17,25},{..., dimensions={0}, use_global_device_ids=true | all-gather | bytes 196608 | tf_op jit(solution)/shard_map/all_gather | solution.py:201
  15.7 17.2 %all-gather.1 = bf16[256,1,1024]{2,0,1:T(8,128)(2,1)S(1)} all-gather(bf16[64,1,1024]{2,0,1:T(8,128)(2,1)S(1)} %all-gather), channel_id=3, replica_groups={{0,2,4,6},{1,3,5,7},{8,10,12,14},{9,11,13,15},{16,18,20,22},{17,19,21,2..., dimensions={0}, use_global_device_ids=true | all-gather | bytes 655360 | tf_op jit(solution)/shard_map/all_gather | solution.py:202
  32.9 0.7 %collective-permute-start.1 = (bf16[256,1024]{1,0:T(8,128)(2,1)S(1)}, bf16[256,1024]{1,0:T(8,128)(2,1)S(1)}, u32[]{:S(2)}, u32[]{:S(2)}) collective-permute-start(bf16[256,1024]{1,0:T(8,128)(2,1)S(1)} %bitcast.4), channel_id=1, source_target_pairs={{0,0},{1,1},{2,2},{3,3},{8,8},{9,9},{10,10},{11,11},{4,5},{5,4},{6... | collective-permute-start | bytes 1572872 | tf_op jit(solution)/shard_map/ppermute | solution.py:203
  33.6 0.0 collective-permute-done.received_ref
  33.6 0.1 shard_map.38
  33.7 0.5 %shard_map.40.first_ref = f32[32,1024]{1,0:T(8,128)S(1)} custom-call(bf16[256,1024]{1,0:T(8,128)(2,1)S(1)} %bitcast.5, bf16[864,256]{1,0:T(8,128)(2,1)S(1)} %get-tuple-element.15.own_ref.weight_ref), custom_call_target="tpu_custom_call" | custom-call | tf_op jit(solution)/shard_map/pallas_call | solution.py:161
  34.2 0.0 collective-permute-done.1.second_ref.plane_ref
  34.2 0.5 %shard_map.41 = (f32[32,1024]{1,0:T(8,128)S(1)}, f32[64,1024]{1,0:T(8,128)S(1)}) custom-call(bf16[256,1024]{1,0:T(8,128)(2,1)S(1)} %collective-permute-done.1.second_ref.plane_ref, bf16[864,256]{1,0:T(8,128)(2,1)S(1)} %get-tuple-element.16.other_ref.weight_ref, f32[32,1024]{1,0:T(8,128)S(1)} %shard_map.40.first_ref), custom_call_target="tpu_custom_call" | custom-call | tf_op jit(solution)/shard_map/pallas_call | solution.py:161
  34.8 1.9 %collective-permute-start.2 = (f32[64,1024]{1,0:T(8,128)S(1)}, f32[64,1024]{1,0:T(8,128)S(1)}, u32[]{:S(2)}, u32[]{:S(2)}) collective-permute-start(f32[64,1024]{1,0:T(8,128)S(1)} %get-tuple-element.17), channel_id=1, source_target_pairs={{16,32},{17,33},{18,34},{19,35},{24,40},{25,41},{26,42},{27,43},{4... | collective-permute-start | bytes 786440 | tf_op jit(solution)/shard_map/ppermute | solution.py:212
  36.7 0.7 %collective-permute-start.3 = (f32[32,1024]{1,0:T(8,128)S(1)}, f32[32,1024]{1,0:T(8,128)S(1)}, u32[]{:S(2)}, u32[]{:S(2)}) collective-permute-start(f32[32,1024]{1,0:T(8,128)S(1)} %get-tuple-element.19), channel_id=1, source_target_pairs={{20,36},{21,37},{22,38},{23,39},{28,44},{29,45},{30,46},{31,47},{5... | collective-permute-start | bytes 393224 | tf_op jit(solution)/shard_map/ppermute | solution.py:213
  37.4 0.8 %shard_map.39 = f32[64,1024]{1,0:T(8,128)S(1)} custom-call(bf16[256,1024]{1,0:T(8,128)(2,1)S(1)} %bitcast.6, bf16[256,1024]{1,0:T(8,128)(2,1)S(1)} %collective-permute-done.1.second_ref.plane_ref, bf16[864,256]{1,0:T(8,128)(2,1)S(1)} %get-tuple-element.15.own_ref.weight_ref, bf16[864,256]{1,0:T(8,128)(2,1)S(1)} %get-tuple-element.16.other_ref.weight_ref), custom_call_target="tpu_custom_call" | custom-call | tf_op jit(solution)/shard_map/pallas_call | solution.py:161
  38.2 3.4 %all-gather.2 = f32[128,1024]{1,0:T(8,128)S(1)} all-gather(f32[64,1024]{1,0:T(8,128)S(1)} %shard_map.39), channel_id=4, replica_groups={{0,16},{32,48},{64,80},{96,112},{128,144},{160,176},{192,208},{224,240}..., dimensions={0}, use_global_device_ids=true | all-gather | bytes 786432 | tf_op jit(solution)/shard_map/all_gather | solution.py:214
  41.6 0.5 %shard_map.42 = (f32[32,1024]{1,0:T(8,128)S(1)}, f32[32,1024]{1,0:T(8,128)S(1)}) custom-call(bf16[256,1024]{1,0:T(8,128)(2,1)S(1)} %collective-permute-done.1.second_ref.plane_ref, bf16[864,256]{1,0:T(8,128)(2,1)S(1)} %get-tuple-element.16.other_ref.weight_ref, f32[2,64,1024]{2,1,0:T(8,128)S(1)} %bitcast.8), custom_call_target="tpu_custom_call" | custom-call | tf_op jit(solution)/shard_map/pallas_call | solution.py:161
  42.2 2.4 %collective-permute-done.2.next_ref = f32[64,1024]{1,0:T(8,128)S(1)} collective-permute-done((f32[64,1024]{1,0:T(8,128)S(1)}, f32[64,1024]{1,0:T(8,128)S(1)}, u32[]{:S(2)}, u32[]{:S(2)}) %collective-permute-start.2) | collective-permute-done | bytes 262176 | tf_op jit(solution)/shard_map/ppermute | solution.py:212
  44.6 3.3 %collective-permute-start.4 = (f32[32,1024]{1,0:T(8,128)S(1)}, f32[32,1024]{1,0:T(8,128)S(1)}, u32[]{:S(2)}, u32[]{:S(2)}) collective-permute-start(f32[32,1024]{1,0:T(8,128)S(1)} %shard_map.44), channel_id=1, source_target_pairs={{0,1},{1,0},{2,3},{3,2},{8,9},{9,8},{10,11},{11,10},{16,17},{17,16... | collective-permute-start | bytes 393224 | tf_op jit(solution)/shard_map/ppermute | solution.py:220
  48.0 0.0 copy-start.1
  48.0 0.5 %shard_map.43 = f32[32,1024]{1,0:T(8,128)S(1)} custom-call(bf16[256,1024]{1,0:T(8,128)(2,1)S(1)} %bitcast.7, bf16[864,256]{1,0:T(8,128)(2,1)S(1)} %get-tuple-element.15.own_ref.weight_ref, f32[2,64,1024]{2,1,0:T(8,128)S(1)} %bitcast.9, f32[64,1024]{1,0:T(8,128)S(1)} %collective-permute-done.2.next_ref, f32[32,1024]{1,0:T(8,128)S(1)} %get-tuple-element.18.second_ref), custom_call_target="tpu_custom_call" | custom-call | tf_op jit(solution)/shard_map/pallas_call | solution.py:161
  48.5 0.0 collective-permute-done.3
  48.5 2.9 %collective-permute-done.4 = f32[32,1024]{1,0:T(8,128)S(1)} collective-permute-done((f32[32,1024]{1,0:T(8,128)S(1)}, f32[32,1024]{1,0:T(8,128)S(1)}, u32[]{:S(2)}, u32[]{:S(2)}) %collective-permute-start.4) | collective-permute-done | bytes 131104 | tf_op jit(solution)/shard_map/ppermute | solution.py:220
  51.5 0.0 copy-done.1
  51.5 0.7 %fusion = bf16[32,1,1024]{2,0,1:T(8,128)(2,1)} fusion(f32[32,1024]{1,0:T(8,128)S(1)} %collective-permute-done.4, f32[32,1024]{1,0:T(8,128)S(1)} %shard_map.43, f32[32,1024]{1,0:T(8,128)S(1)} %collective-permute-done.3, f32[32]{0:T(128)S(1)} %copy-done.1), kind=kLoop, calls=%fused_computation.1 | loop fusion | flops 131072 | bytes 458880 | tf_op jit(solution)/shard_map/convert_element_type | solution.py:223
  (1 shorter events, 0.0 us)
Async XLA Ops:
  0.0 6.2 %copy-start = (bf16[32,1,1024]{2,0,1:T(8,128)(2,1)S(1)}, bf16[32,1,1024]{2,0,1:T(8,128)(2,1)}, u32[]{:S(2)}) copy-start(bf16[32,1,1024]{2,0,1:T(8,128)(2,1)} %param.3) | copy-start | bytes 196612
  1.9 31.7 %collective-permute-start = (bf16[864,256]{1,0:T(8,128)(2,1)S(1)}, bf16[864,256]{1,0:T(8,128)(2,1)S(1)}, u32[]{:S(2)}, u32[]{:S(2)}) collective-permute-start(bf16[864,256]{1,0:T(8,128)(2,1)S(1)} %get-tuple-element.14), channel_id=1, source_target_pairs={{0,1},{1,0},{2,3},{3,2},{8,9},{9,8},{10,11},{11,10},{16,17},{17,16... | collective-permute-start | bytes 1327112 | tf_op jit(solution)/shard_map/ppermute | solution.py:199
  32.9 1.3 %collective-permute-start.1 = (bf16[256,1024]{1,0:T(8,128)(2,1)S(1)}, bf16[256,1024]{1,0:T(8,128)(2,1)S(1)}, u32[]{:S(2)}, u32[]{:S(2)}) collective-permute-start(bf16[256,1024]{1,0:T(8,128)(2,1)S(1)} %bitcast.4), channel_id=1, source_target_pairs={{0,0},{1,1},{2,2},{3,3},{8,8},{9,9},{10,10},{11,11},{4,5},{5,4},{6... | collective-permute-start | bytes 1572872 | tf_op jit(solution)/shard_map/ppermute | solution.py:203
  34.8 9.8 %collective-permute-start.2 = (f32[64,1024]{1,0:T(8,128)S(1)}, f32[64,1024]{1,0:T(8,128)S(1)}, u32[]{:S(2)}, u32[]{:S(2)}) collective-permute-start(f32[64,1024]{1,0:T(8,128)S(1)} %get-tuple-element.17), channel_id=1, source_target_pairs={{16,32},{17,33},{18,34},{19,35},{24,40},{25,41},{26,42},{27,43},{4... | collective-permute-start | bytes 786440 | tf_op jit(solution)/shard_map/ppermute | solution.py:212
  36.7 11.8 %collective-permute-start.3 = (f32[32,1024]{1,0:T(8,128)S(1)}, f32[32,1024]{1,0:T(8,128)S(1)}, u32[]{:S(2)}, u32[]{:S(2)}) collective-permute-start(f32[32,1024]{1,0:T(8,128)S(1)} %get-tuple-element.19), channel_id=1, source_target_pairs={{20,36},{21,37},{22,38},{23,39},{28,44},{29,45},{30,46},{31,47},{5... | collective-permute-start | bytes 393224 | tf_op jit(solution)/shard_map/ppermute | solution.py:213
  44.6 6.9 %collective-permute-start.4 = (f32[32,1024]{1,0:T(8,128)S(1)}, f32[32,1024]{1,0:T(8,128)S(1)}, u32[]{:S(2)}, u32[]{:S(2)}) collective-permute-start(f32[32,1024]{1,0:T(8,128)S(1)} %shard_map.44), channel_id=1, source_target_pairs={{0,1},{1,0},{2,3},{3,2},{8,9},{9,8},{10,11},{11,10},{16,17},{17,16... | collective-permute-start | bytes 393224 | tf_op jit(solution)/shard_map/ppermute | solution.py:220
  48.0 3.5 %copy-start.1 = (f32[32]{0:T(128)S(1)}, f32[32]{0:T(128)}, u32[]{:S(2)}) copy-start(f32[32]{0:T(128)} %param.5) | copy-start | bytes 388
